TPU v7x, 32 devices: a whole 2x2x4 slice. The times are simulated.
32 devices in a mesh: section: 2 (over x), ctx: 8 (over z, y), tp: 2 (over core).
Axes of the slice: x: 2, y: 2, z: 4, core: 2. Of those that a mesh axis runs over, the one named last changes fastest.
Arguments:
- tokens: bfloat16 [4, 2048, 1024], P(None, 'ctx'), may hold values from -6 to 6
- cotangent: bfloat16 [4, 2048, 1024], P(None, 'ctx'), may hold values from -6 to 6
- block_order: int32 [16], replicated, may hold values from 0 to 15, each once
- first_gain: float32 [2, 1024], P('section'), may hold values from 0.25 to 1.75
- first_bias: float32 [2, 1024], P('section'), may hold values from -1.75 to 1.75
- second_gain: float32 [2, 1024], P('section'), may hold values from 0.25 to 1.75
- second_bias: float32 [2, 1024], P('section'), may hold values from -1.75 to 1.75
- joint_weight: bfloat16 [2, 3, 1024, 1024], P('section', None, None, 'tp'), may hold values from -0.25 to 0.25
- joint_bias: float32 [2, 3, 1024], P('section', None, 'tp'), may hold values from -1.75 to 1.75
- output_weight: bfloat16 [2, 1024, 1024], P('section', 'tp'), may hold values from -0.5 to 0.5
- output_bias: float32 [2, 1024], P('section'), may hold values from -1.75 to 1.75
- up_weight: bfloat16 [2, 1024, 4096], P('section', None, 'tp'), may hold values from -0.1875 to 0.1875
- up_bias: float32 [2, 4096], P('section', 'tp'), may hold values from -1.75 to 1.75
- down_weight: bfloat16 [2, 4096, 1024], P('section', 'tp'), may hold values from -0.125 to 0.125
- down_bias: float32 [2, 1024], P('section'), may hold values from -1.75 to 1.75
Outputs:
- section_out: bfloat16 [2, 4, 2048, 1024], P('section', None, 'ctx')
- section_in_grad: bfloat16 [2, 4, 2048, 1024], P('section', None, 'ctx')
- first_gain_gradient: float32 [2, 1024], P('section')
- first_bias_gradient: float32 [2, 1024], P('section')
- second_gain_gradient: float32 [2, 1024], P('section')
- second_bias_gradient: float32 [2, 1024], P('section')
- joint_weight_gradient: float32 [2, 3, 1024, 1024], P('section', None, 'ctx', 'tp')
- joint_bias_gradient: float32 [2, 3, 1024], P('section', None, 'tp')
- output_weight_gradient: float32 [2, 1024, 1024], P('section', 'tp', 'ctx')
- output_bias_gradient: float32 [2, 1024], P('section')
- up_weight_gradient: float32 [2, 1024, 4096], P('section', 'ctx', 'tp')
- up_bias_gradient: float32 [2, 4096], P('section', 'tp')
- down_weight_gradient: float32 [2, 4096, 1024], P('section', 'tp', 'ctx')
- down_bias_gradient: float32 [2, 1024], P('section')
- root_means: float32 [2, 3], P('section')
Inputs may be any that keep to these rules, and one draw needn't show every extreme that they name: `block_order`: each stored block's place in its sequence, every place once; the same for all sequences.
All inputs are finite; a program needn't handle non-finite values.
Results may differ from a plain program's by a relative error of at most 0.028.
Values may be sent and summed in bfloat16 or wider, within the bound.
A program may use at most 256 MiB of HBM per device.

v0:
```python
import functools

import jax
import jax.numpy as jnp
from jax import lax
from jax.experimental import pallas as pl
from jax.experimental.pallas import tpu as pltpu
from jax.sharding import PartitionSpec as P

HEAD = 64
ROT = 16
EPS = 1e-05
ROTARY_BASE = 10000.0
NEGATIVE = -1e30
STACK = 4
GROUP = STACK * HEAD
KEY_TILE = 512
VMEM_LIMIT = 60 * 1024 * 1024
BF16 = jnp.bfloat16
F32 = jnp.float32


def dot(a, b):
    return jnp.dot(a, b, preferred_element_type=F32)


def dot_nt(a, b):
    return lax.dot_general(a, b, (((1,), (1,)), ((), ())), preferred_element_type=F32)


def params_of(**more):
    return pltpu.CompilerParams(vmem_limit_bytes=VMEM_LIMIT, **more)


def whole(shape):
    return pl.BlockSpec(shape, lambda *_: (0,) * len(shape))


def rows_of(tile, *rest):
    return pl.BlockSpec((tile, *rest), lambda r, *_: (r,) + (0,) * len(rest))


def halves_of(tile, count, *rest):
    return [
        pl.BlockSpec((tile, *rest), lambda r, *_: (jnp.minimum(r, count - 1),) + (0,) * len(rest)),
        pl.BlockSpec((tile, *rest), lambda r, *_: (jnp.maximum(r - count, 0),) + (0,) * len(rest)),
    ]


def pick(refs):
    return jnp.where(pl.program_id(0) < pl.num_programs(0) // 2, refs[0][...], refs[1][...])


def put(refs, value):
    first = pl.program_id(0) < pl.num_programs(0) // 2
    for ref, here in zip(refs, (first, jnp.logical_not(first))):

        @pl.when(here)
        def _():
            ref[...] = value


def waiting(kernel, inputs, deps):
    return lambda *refs: kernel(*refs[:inputs], *refs[inputs + len(deps) :])


def exchanged(position, mask):
    for bit in range(mask.bit_length()):
        if mask >> bit & 1:
            position = position + (1 << bit) - (2 << bit) * (position // (1 << bit) % 2)
    return position


def carrying(kernel, inputs, outputs, moves):
    count = len(moves)

    def body(*refs):
        sources = refs[inputs : inputs + count]
        outs = refs[inputs + count : inputs + count + outputs]
        targets = refs[inputs + count + outputs : inputs + 2 * count + outputs]
        *scratch, send, receive = refs[inputs + 2 * count + outputs :]
        partners = [{axis: exchanged(lax.axis_index(axis), mask)} for axis, mask in moves]
        copies = [
            pltpu.make_async_remote_copy(
                source, target, send.at[n], receive.at[n], device_id=partner, device_id_type=pl.DeviceIdType.MESH
            )
            for n, (source, target, partner) in enumerate(zip(sources, targets, partners))
        ]

        @pl.when(pl.program_id(0) == 0)
        def _():
            barrier = pltpu.get_barrier_semaphore()
            for partner in partners:
                pl.semaphore_signal(barrier, inc=1, device_id=partner, device_id_type=pl.DeviceIdType.MESH)
            pl.semaphore_wait(barrier, count)
            for copy in copies:
                copy.start()

        kernel(*refs[:inputs], *outs, *scratch)

        @pl.when(pl.program_id(0) == pl.num_programs(0) - 1)
        def _():
            for copy in copies:
                copy.wait()

    return body


def carrier_semaphores(count):
    return [pltpu.SemaphoreType.DMA((count,)), pltpu.SemaphoreType.DMA((count,))]


def anywhere(count):
    return [pl.BlockSpec(memory_space=pl.ANY)] * count


def cost(flops, size):
    return pl.CostEstimate(flops=int(flops), bytes_accessed=int(size), transcendentals=0)


def shape_of(*shape, dtype=BF16):
    return jax.ShapeDtypeStruct(shape, dtype)


def normalize(values):
    middle = jnp.mean(values, axis=-1, keepdims=True)
    centered = values - middle
    spread = jnp.mean(centered * centered, axis=-1, keepdims=True)
    inverse = lax.rsqrt(spread + EPS)
    return centered * inverse, inverse


def turn(values, cosine, sine):
    pieces = []
    for start in range(0, values.shape[1], 128):
        part = values[:, start : start + 128]
        ahead = pltpu.roll(part, 128 - ROT // 2, 1)
        behind = pltpu.roll(part, ROT // 2, 1)
        entry = lax.broadcasted_iota(jnp.int32, part.shape, 1) % HEAD
        pieces.append(part * cosine + jnp.where(entry < ROT // 2, -ahead, behind) * sine)
    return jnp.concatenate(pieces, axis=1)


def joint_kernel(h0_ref, h1_ref, gain_ref, shift_ref, w_ref, b_ref, cos_ref, sin_ref, n_ref, k_ref, v_ref):
    scaled, _ = normalize(pick((h0_ref, h1_ref)).astype(F32))
    low = (scaled * gain_ref[...] + shift_ref[...]).astype(BF16)
    n_ref[...] = low
    cosine, sine = cos_ref[...], sin_ref[...]
    keys = dot(low, w_ref[1]) + b_ref[1:2]
    values = dot(low, w_ref[2]) + b_ref[2:3]
    k_ref[...] = turn(keys, cosine, sine).astype(BF16)
    v_ref[...] = values.astype(BF16)


def joint_call(pair, gain, shift, w_joint, b_joint, table, offset, deps=()):
    rows, width = pair[0].shape
    local = w_joint.shape[2]
    tile = min(512, rows)
    first = offset // tile
    count = 2
    turns = pl.BlockSpec((tile, 128), lambda r: (first + r, 0))
    return pl.pallas_call(
        waiting(joint_kernel, 8, deps),
        grid=(2 * rows // tile,),
        in_specs=halves_of(tile, rows // tile, width)
        + [whole((1, width)), whole((1, width)), whole(w_joint.shape), whole(b_joint.shape), turns, turns]
        + anywhere(len(deps)),
        out_specs=[rows_of(tile, width)] + [rows_of(tile, local)] * count,
        out_shape=[shape_of(2 * rows, width)] + [shape_of(2 * rows, local)] * count,
        compiler_params=params_of(),
        cost_estimate=cost(4 * rows * width * local * count, 8 * rows * width + 2 * w_joint.size),
        name="joint_projection",
    )(*pair, gain, shift, w_joint, b_joint, *table, *deps)


def gelu_parts(x):
    return 0.5 + 0.5 * lax.erf(x * 0.5**0.5), jnp.exp(-0.5 * x * x)


def front_kernel(
    save, h0_ref, h1_ref, norms_ref, w_ref, b_ref, cos_ref, sin_ref, up_ref, up_b_ref, down_ref,
    n_ref, k_ref, v_ref, q_ref, part0_ref, part1_ref, *saved
):
    scaled, _ = normalize(pick((h0_ref, h1_ref)).astype(F32))
    low = (scaled * norms_ref[0:1] + norms_ref[1:2]).astype(BF16)
    n_ref[...] = low
    cosine, sine = cos_ref[...], sin_ref[...]
    keys = dot(low, w_ref[1]) + b_ref[1:2]
    values = dot(low, w_ref[2]) + b_ref[2:3]
    queries = dot(low, w_ref[0]) + b_ref[0:1]
    q_ref[...] = (turn(queries, cosine, sine) * HEAD ** (-0.5)).astype(BF16)
    k_ref[...] = turn(keys, cosine, sine).astype(BF16)
    v_ref[...] = values.astype(BF16)
    low = (scaled * norms_ref[2:3] + norms_ref[3:4]).astype(BF16)
    if save:
        saved[0][...] = low
    total = None
    for start in range(0, up_ref.shape[1], 512):
        cut = pl.ds(start, 512)
        hidden = dot(low, up_ref[:, cut]) + up_b_ref[:, cut]
        share, bell = gelu_parts(hidden)
        active = (hidden * share).astype(BF16)
        if save:
            saved[1][:, cut] = active
            saved[2][:, cut] = (share + hidden * bell * 0.3989422804014327).astype(BF16)
        term = dot(active, down_ref[cut, :])
        total = term if total is None else total + term
    put((part0_ref, part1_ref), total.astype(BF16))


def front_call(pair, norms, w_joint, b_joint, table, w_up, b_up, w_down, save, moves, moved, name, number):
    rows, width = pair[0].shape
    local = w_joint.shape[2]
    units = w_up.shape[1]
    tile = min(512, rows)
    out = [shape_of(2 * rows, width)] + [shape_of(2 * rows, local)] * 3 + [shape_of(rows, width)] * 2
    out_specs = [rows_of(tile, width)] + [rows_of(tile, local)] * 3 + halves_of(tile, rows // tile, width)
    if save:
        out += [shape_of(2 * rows, width)] + [shape_of(2 * rows, units)] * 2
        out_specs += [rows_of(tile, width), rows_of(tile, units), rows_of(tile, units)]
    ins = (norms, w_joint, b_joint, *table, w_up, b_up, w_down)
    turns = rows_of(tile, 128)
    specs = [turns if x is table[0] or x is table[1] else whole(x.shape) for x in ins]
    outs = pl.pallas_call(
        carrying(functools.partial(front_kernel, save), 2 + len(ins), len(out), moves),
        grid=(2 * rows // tile,),
        in_specs=halves_of(tile, rows // tile, width) + specs + anywhere(len(moves)),
        out_specs=out_specs + anywhere(len(moves)),
        out_shape=out + [shape_of(*x.shape) for x in moved],
        scratch_shapes=carrier_semaphores(len(moves)),
        compiler_params=params_of(collective_id=number, has_side_effects=True),
        cost_estimate=cost(4 * rows * width * (3 * local + 2 * units), 4 * w_up.size + 16 * rows * width),
        name=name,
    )(*pair, *ins, *moved)
    return outs[: len(out)], outs[len(out) :]


def ffn_back_kernel(g0_ref, g1_ref, slope_ref, up_ref, down_ref, part0_ref, part1_ref, hidden_ref, sums_ref):
    upstream = pick((g0_ref, g1_ref))
    units = up_ref.shape[1]

    @pl.when(pl.program_id(0) == 0)
    def _():
        sums_ref[...] = jnp.zeros_like(sums_ref)

    total = None
    for start in range(0, units, 512):
        cut = pl.ds(start, 512)
        d_active = dot_nt(upstream, down_ref[cut, :])
        d_hidden = (d_active * slope_ref[:, cut].astype(F32)).astype(BF16)
        hidden_ref[:, cut] = d_hidden
        sums_ref[:, cut] += jnp.sum(d_hidden.astype(F32), axis=0, keepdims=True)
        term = dot_nt(d_hidden, up_ref[:, cut])
        total = term if total is None else total + term
    put((part0_ref, part1_ref), total.astype(BF16))


def ffn_back_call(pair, slope, w_up, w_down, deps=()):
    rows, width = pair[0].shape
    units = w_up.shape[1]
    tile = min(512, rows)
    return pl.pallas_call(
        waiting(ffn_back_kernel, 5, deps),
        grid=(2 * rows // tile,),
        in_specs=halves_of(tile, rows // tile, width) + [rows_of(tile, units), whole(w_up.shape), whole(w_down.shape)]
        + anywhere(len(deps)),
        out_specs=halves_of(tile, rows // tile, width) + [rows_of(tile, units), whole((1, units))],
        out_shape=[shape_of(rows, width)] * 2 + [shape_of(2 * rows, units), shape_of(1, units, dtype=F32)],
        compiler_params=params_of(),
        cost_estimate=cost(8 * rows * width * units, 4 * w_up.size + 8 * rows * (width + units)),
        name="feed_forward_back",
    )(*pair, slope, w_up, w_down, *deps)


def start_sorted(places_ref, parts, targets, sem, block):
    copies = []
    for refs, target in zip(parts, targets):
        index = 0
        for ref in refs:
            for local in range(ref.shape[0] // block):
                place = pl.ds(pl.multiple_of(places_ref[index] * block, block), block)
                copies.append(pltpu.make_async_copy(ref.at[pl.ds(local * block, block)], target.at[place], sem))
                index += 1
    for copy in copies:
        copy.start()
    return copies


def transpose_into(source, target):
    rows, columns = source.shape

    def step(index, _):
        start = pl.multiple_of(index * 256, 256)
        for column in range(0, columns, 256):
            target[column : column + 256, pl.ds(start, 256)] = source[pl.ds(start, 256), column : column + 256].T
        return 0

    lax.fori_loop(0, rows // 256, step, 0)


def stacked(values):
    owner = lax.broadcasted_iota(jnp.int32, values.shape, 1) // HEAD
    zero = jnp.zeros_like(values)
    return jnp.concatenate([jnp.where(owner == a, values, zero) for a in range(STACK)], axis=0)


def spots_of(places_ref, step, tile, block, shape, axis):
    at = lax.broadcasted_iota(jnp.int32, shape, axis) % tile
    count = tile // block
    spot = at + places_ref[step * count] * block
    for s in range(1, count):
        spot = jnp.where(at >= s * block, at - s * block + places_ref[step * count + s] * block, spot)
    return spot


def attend_kernel(block, tile, remote, places_ref, limits_ref, q_ref, wo_ref, *refs):
    key_refs, value_refs = refs[: 1 + remote], refs[1 + remote : 2 + 2 * remote]
    part0_ref, part1_ref, mix_ref, lse_ref, keys, values, scores_ref, sem = refs[2 + 2 * remote :]
    groups = q_ref.shape[1] // GROUP
    half = part0_ref.shape[0]
    rows = STACK * tile
    lanes = [slice(g * GROUP, (g + 1) * GROUP) for g in range(groups)]
    for copy in start_sorted(places_ref, (key_refs, value_refs), (keys, values), sem, block):
        copy.wait()

    def tile_step(step, _):
        mine = pl.ds(pl.multiple_of(step * tile, tile), tile)
        heads = [stacked(q_ref[mine, lane]) for lane in lanes]
        spots = spots_of(places_ref, step, tile, block, (rows, 128), 0)

        def attend_to(count):
            open_end = (count - 1) * KEY_TILE if tile == block else 0
            tops = []
            for g, lane in enumerate(lanes):
                top = None
                for start in range(0, count * KEY_TILE, KEY_TILE):
                    scores = dot_nt(heads[g], keys[start : start + KEY_TILE, lane])
                    for column in range(0, KEY_TILE, 128):
                        piece = scores[:, column : column + 128]
                        if start + column >= open_end:
                            spot = start + column + lax.broadcasted_iota(jnp.int32, piece.shape, 1)
                            piece = jnp.where(spot <= spots, piece, NEGATIVE)
                        scores_ref[g, :, start + column : start + column + 128] = piece
                        top = piece if top is None else jnp.maximum(top, piece)
                tops.append(jnp.broadcast_to(jnp.max(top, axis=1, keepdims=True), (rows, 128)))
            for g, lane in enumerate(lanes):
                mass, total = None, None
                for start in range(0, count * KEY_TILE, KEY_TILE):
                    raised = []
                    for column in range(start, start + KEY_TILE, 128):
                        piece = jnp.exp(scores_ref[g, :, column : column + 128] - tops[g])
                        mass = piece if mass is None else mass + piece
                        raised.append(piece.astype(BF16))
                    term = dot(jnp.concatenate(raised, axis=1), values[start : start + KEY_TILE, lane])
                    total = term if total is None else total + term
                mass = jnp.broadcast_to(jnp.sum(mass, axis=1, keepdims=True), (rows, 128))
                total = total * jnp.concatenate([1.0 / mass] * (GROUP // 128), axis=1)
                owner = lax.broadcasted_iota(jnp.int32, (tile, GROUP), 1) // HEAD
                mixture = total[:tile]
                for a in range(1, STACK):
                    mixture = jnp.where(owner == a, total[a * tile : (a + 1) * tile], mixture)
                mix_ref[mine, lane] = mixture.astype(BF16)
                lse = tops[g] + jnp.log(mass)
                for a in range(STACK):
                    lse_ref[step, g : g + 1, a * tile : (a + 1) * tile] = lse[a * tile : (a + 1) * tile].T[0:1]

        for count in range(1, keys.shape[0] // KEY_TILE + 1):
            pl.when(limits_ref[step, 1] == count)(functools.partial(attend_to, count))
        return 0

    lax.fori_loop(0, q_ref.shape[0] // tile, tile_step, 0)
    part0_ref[...] = dot(mix_ref[:half], wo_ref[...]).astype(BF16)
    part1_ref[...] = dot(mix_ref[half:], wo_ref[...]).astype(BF16)


def attend_call(queries, key_parts, value_parts, places, limits, w_output, block, deps=()):
    rows, local = queries.shape
    width = w_output.shape[1]
    tile = rows // limits.shape[0]
    length = sum(part.shape[0] for part in key_parts)
    groups = local // GROUP
    outs = [(rows // 2, width), (rows // 2, width), (rows, local), (rows // tile, groups, STACK * tile)]
    return pl.pallas_call(
        waiting(functools.partial(attend_kernel, block, tile, len(key_parts) - 1), 4 + 2 * len(key_parts), deps),
        grid_spec=pltpu.PrefetchScalarGridSpec(
            num_scalar_prefetch=2,
            grid=(1,),
            in_specs=[whole((rows, local)), whole(w_output.shape)] + anywhere(2 * len(key_parts) + len(deps)),
            out_specs=[whole(shape) for shape in outs],
            scratch_shapes=[
                pltpu.VMEM((length, local), BF16),
                pltpu.VMEM((length, local), BF16),
                pltpu.VMEM((groups, STACK * tile, length), F32),
                pltpu.SemaphoreType.DMA,
            ],
        ),
        out_shape=[shape_of(*shape) for shape in outs[:3]] + [shape_of(*outs[3], dtype=F32)],
        compiler_params=params_of(),
        cost_estimate=cost(12 * rows * length * local, 2 * length * local * 4),
        name="attend",
    )(places, limits, queries, w_output, *key_parts, *value_parts, *deps)


def attend_back_kernel(
    block, tile, remote, places_ref, limits_ref, q_ref, g0_ref, g1_ref, mix_ref, lse_ref, wo_ref, cos_ref, sin_ref, *refs
):
    key_refs, value_refs = refs[: 1 + remote], refs[1 + remote : 2 + 2 * remote]
    (dq_ref, dk_ref, dv_ref, sums_ref, keys, values, keys_t, d_keys, d_values, d_mixture, inner, total, d_queries, sem) = refs[
        2 + 2 * remote :
    ]
    groups = q_ref.shape[1] // GROUP
    rows = q_ref.shape[0]
    half = g0_ref.shape[0]
    lanes = [slice(g * GROUP, (g + 1) * GROUP) for g in range(groups)]
    copies = start_sorted(places_ref, (key_refs, value_refs), (keys, values), sem, block)
    d_keys[...] = jnp.zeros_like(d_keys)
    d_values[...] = jnp.zeros_like(d_values)
    head_of = lax.broadcasted_iota(jnp.int32, (8, GROUP), 1) // HEAD
    picker = jnp.where(lax.broadcasted_iota(jnp.int32, (8, GROUP), 0) == head_of, 1.0, 0.0).astype(BF16)
    for index, ref in enumerate((g0_ref, g1_ref)):
        cut = pl.ds(index * half, half)
        low = dot_nt(ref[...], wo_ref[...]).astype(BF16)
        d_mixture[cut, :] = low
        product = low.astype(F32) * mix_ref[cut, :].astype(F32)
        high = product.astype(BF16)
        rest = (product - high.astype(F32)).astype(BF16)
        for g, lane in enumerate(lanes):
            inner[g * 8 : (g + 1) * 8, cut] = dot_nt(picker, high[:, lane]) + dot_nt(picker, rest[:, lane])
    for copy in copies:
        copy.wait()
    transpose_into(keys, keys_t)

    def query_step(step, _):
        mine = pl.ds(pl.multiple_of(step * tile, tile), tile)
        spots = spots_of(places_ref, step, tile, block, (1, STACK * tile), 1)
        heads = [stacked(q_ref[mine, lane]) for lane in lanes]
        sides = [stacked(d_mixture[mine, lane]) for lane in lanes]
        sums = [
            jnp.concatenate([inner[g * 8 + a : g * 8 + a + 1, mine] for a in range(STACK)], axis=1) for g in range(groups)
        ]
        lse = [lse_ref[step, g : g + 1, :] for g in range(groups)]
        total[...] = jnp.zeros_like(total)

        def key_step(masked, index, carry):
            start = pl.multiple_of(index * KEY_TILE, KEY_TILE)
            cut = pl.ds(start, KEY_TILE)
            for g, lane in enumerate(lanes):
                scores = dot_nt(keys[cut, lane], heads[g])
                if masked:
                    spot = start + lax.broadcasted_iota(jnp.int32, scores.shape, 0)
                    scores = jnp.where(spot <= spots, scores, NEGATIVE)
                weights = jnp.exp(scores - lse[g])
                d_weights = dot_nt(values[cut, lane], sides[g])
                d_scores = (weights * (d_weights - sums[g])).astype(BF16)
                d_values[cut, lane] += dot(weights.astype(BF16), sides[g])
                d_keys[cut, lane] += dot(d_scores, heads[g])
                total[lane, :] += dot(keys_t[lane, cut], d_scores)
            return carry

        lax.fori_loop(0, limits_ref[step, 0], functools.partial(key_step, False), 0)
        lax.fori_loop(limits_ref[step, 0], limits_ref[step, 1], functools.partial(key_step, True), 0)
        for lane in lanes:
            picked = [total[lane, :][a * HEAD : (a + 1) * HEAD, a * tile : (a + 1) * tile] for a in range(STACK)]
            d_queries[mine, lane] = jnp.concatenate(picked, axis=0).T
        return 0

    lax.fori_loop(0, rows // tile, query_step, 0)
    turned = turn(d_queries[...] * HEAD ** (-0.5), cos_ref[:rows], -sin_ref[:rows]).astype(BF16)
    dq_ref[...] = turned
    sums_ref[...] = jnp.zeros_like(sums_ref)
    sums_ref[0:1, :] = jnp.sum(turned.astype(F32), axis=0, keepdims=True)

    def block_step(index, _):
        place = pl.ds(pl.multiple_of(places_ref[index] * block, block), block)
        mine = pl.ds(pl.multiple_of(index * block, block), block)
        turned = turn(d_keys[place, :], cos_ref[mine, :], -sin_ref[mine, :]).astype(BF16)
        dk_ref[mine, :] = turned
        low = d_values[place, :].astype(BF16)
        dv_ref[mine, :] = low
        sums_ref[1:2, :] += jnp.sum(turned.astype(F32), axis=0, keepdims=True)
        sums_ref[2:3, :] += jnp.sum(low.astype(F32), axis=0, keepdims=True)
        return 0

    lax.fori_loop(0, dk_ref.shape[0] // block, block_step, 0)


def attend_back_call(
    queries, g_pair, mixture, lse, key_parts, value_parts, places, limits, w_output, table, block, deps=()
):
    rows, local = queries.shape
    width = w_output.shape[1]
    tile = rows // limits.shape[0]
    length = sum(part.shape[0] for part in key_parts)
    groups = local // GROUP
    ins = (queries, *g_pair, mixture, lse, w_output, *table)
    return pl.pallas_call(
        waiting(
            functools.partial(attend_back_kernel, block, tile, len(key_parts) - 1), 2 + len(ins) + 2 * len(key_parts), deps
        ),
        grid_spec=pltpu.PrefetchScalarGridSpec(
            num_scalar_prefetch=2,
            grid=(1,),
            in_specs=[whole(x.shape) for x in ins] + anywhere(2 * len(key_parts) + len(deps)),
            out_specs=[whole((rows, local)), whole((length, local)), whole((length, local)), whole((8, local))],
            scratch_shapes=[
                pltpu.VMEM((length, local), BF16),
                pltpu.VMEM((length, local), BF16),
                pltpu.VMEM((local, length), BF16),
                pltpu.VMEM((length, local), F32),
                pltpu.VMEM((length, local), F32),
                pltpu.VMEM((rows, local), BF16),
                pltpu.VMEM((8 * groups, rows), F32),
                pltpu.VMEM((local, STACK * tile), F32),
                pltpu.VMEM((rows, local), F32),
                pltpu.SemaphoreType.DMA,
            ],
        ),
        out_shape=[shape_of(rows, local), shape_of(length, local), shape_of(length, local), shape_of(8, local, dtype=F32)],
        compiler_params=params_of(),
        cost_estimate=cost(24 * rows * length * local, 2 * length * local * 8),
        name="attend_back",
    )(places, limits, *ins, *key_parts, *value_parts, *deps)


def joint_back_kernel(count, *refs):
    w_ref = refs[count]
    total = None
    for index in range(count):
        term = dot_nt(refs[index][...], w_ref[3 - count + index])
        total = term if total is None else total + term
    put(refs[count + 1 :], total.astype(BF16))


def joint_back_call(grads, offset, rows, w_joint, deps=()):
    width, local = w_joint.shape[1:]
    half = rows // 2
    tile = min(512, half)
    first = offset // tile
    return pl.pallas_call(
        waiting(functools.partial(joint_back_kernel, len(grads)), len(grads) + 1, deps),
        grid=(rows // tile,),
        in_specs=[pl.BlockSpec((tile, local), lambda r: (first + r, 0))] * len(grads)
        + [whole(w_joint.shape)]
        + anywhere(len(deps)),
        out_specs=halves_of(tile, half // tile, width),
        out_shape=[shape_of(half, width)] * 2,
        compiler_params=params_of(),
        cost_estimate=cost(2 * rows * width * local * len(grads), 2 * rows * (width + 3 * local) + 2 * w_joint.size),
        name="joint_projection_back",
    )(*grads, w_joint, *deps)


def rear_kernel(q_ref, k_ref, v_ref, w_ref, g0_ref, g1_ref, slope_ref, up_ref, down_ref, first0_ref, first1_ref, part0_ref, part1_ref):
    total = dot_nt(q_ref[...], w_ref[0]) + dot_nt(k_ref[...], w_ref[1]) + dot_nt(v_ref[...], w_ref[2])
    put((first0_ref, first1_ref), total.astype(BF16))
    upstream = pick((g0_ref, g1_ref))
    total = None
    for start in range(0, up_ref.shape[1], 512):
        cut = pl.ds(start, 512)
        d_active = dot_nt(upstream, down_ref[cut, :])
        d_hidden = (d_active * slope_ref[:, cut].astype(F32)).astype(BF16)
        term = dot_nt(d_hidden, up_ref[:, cut])
        total = term if total is None else total + term
    put((part0_ref, part1_ref), total.astype(BF16))


def rear_call(grads, w_joint, pair, slope, w_up, w_down, moves, moved, name, number):
    rows, width = pair[0].shape
    local = w_joint.shape[2]
    units = w_up.shape[1]
    tile = min(512, rows)
    halves = halves_of(tile, rows // tile, width)
    outs = pl.pallas_call(
        carrying(rear_kernel, 9, 4, moves),
        grid=(2 * rows // tile,),
        in_specs=[rows_of(tile, local)] * 3
        + [whole(w_joint.shape)]
        + halves
        + [rows_of(tile, units), whole(w_up.shape), whole(w_down.shape)]
        + anywhere(len(moves)),
        out_specs=halves + halves + anywhere(len(moves)),
        out_shape=[shape_of(rows, width)] * 4 + [shape_of(*x.shape) for x in moved],
        scratch_shapes=carrier_semaphores(len(moves)),
        compiler_params=params_of(collective_id=number, has_side_effects=True),
        cost_estimate=cost(4 * rows * width * (3 * local + 2 * units), 4 * w_up.size + 16 * rows * width),
        name=name,
    )(*grads, w_joint, *pair, slope, w_up, w_down, *moved)
    return outs[:2], outs[2:4], outs[4:]


def norm_back_kernel(firsts, h_ref, g_ref, gains_ref, *refs):
    first_refs, second_refs, (out_ref, sums_ref) = refs[:firsts], refs[firsts:-2], refs[-2:]

    @pl.when(pl.program_id(0) == 0)
    def _():
        sums_ref[...] = jnp.zeros_like(sums_ref)

    scaled, inverse = normalize(h_ref[...].astype(F32))
    upstream = g_ref[...].astype(F32)
    d_first = sum(ref[...].astype(F32) for ref in first_refs)
    d_second = sum(ref[...].astype(F32) for ref in second_refs)
    for row, term in enumerate((d_first * scaled, d_first, d_second * scaled, d_second, upstream)):
        sums_ref[row : row + 1, :] += jnp.sum(term, axis=0, keepdims=True)
    d_scaled = d_first * gains_ref[0:1] + d_second * gains_ref[1:2]
    middle = jnp.mean(d_scaled, axis=-1, keepdims=True)
    along = jnp.mean(d_scaled * scaled, axis=-1, keepdims=True)
    out_ref[...] = (upstream + inverse * (d_scaled - middle - scaled * along)).astype(BF16)


def norm_back_call(h, g, firsts, seconds, gains, deps=()):
    rows, width = h.shape
    tile = min(128, rows)
    one = rows_of(tile, width)
    return pl.pallas_call(
        waiting(functools.partial(norm_back_kernel, len(firsts)), 3 + len(firsts) + len(seconds), deps),
        grid=(rows // tile,),
        in_specs=[one, one, whole(gains.shape)] + [one] * (len(firsts) + len(seconds)) + anywhere(len(deps)),
        out_specs=[one, whole((8, width))],
        out_shape=[shape_of(rows, width), shape_of(8, width, dtype=F32)],
        compiler_params=params_of(),
        cost_estimate=cost(20 * rows * width, 2 * rows * width * 8),
        name="norm_back",
    )(h, g, gains, *firsts, *seconds, *deps)


def merge_kernel(h_ref, a0_ref, a1_ref, f0_ref, f1_ref, shifts_ref, out_ref, sums_ref):
    @pl.when(pl.program_id(0) == 0)
    def _():
        sums_ref[...] = jnp.zeros_like(sums_ref)

    state = h_ref[...].astype(F32)
    attention = a0_ref[...].astype(F32) + a1_ref[...].astype(F32) + shifts_ref[0:1]
    feedforward = f0_ref[...].astype(F32) + f1_ref[...].astype(F32) + shifts_ref[1:2]
    out_ref[...] = (state + attention + feedforward).astype(BF16)
    for row, term in enumerate((state, attention, feedforward)):
        sums_ref[row : row + 1, :] += jnp.sum(term * term, axis=0, keepdims=True)


def merge_call(h, attn_pair, ffn_pair, shifts, deps=()):
    rows, width = h.shape
    tile = min(128, rows)
    one = rows_of(tile, width)
    return pl.pallas_call(
        waiting(merge_kernel, 6, deps),
        grid=(rows // tile,),
        in_specs=[one] * 5 + [whole(shifts.shape)] + anywhere(len(deps)),
        out_specs=[one, whole((8, width))],
        out_shape=[shape_of(rows, width), shape_of(8, width, dtype=F32)],
        compiler_params=params_of(),
        cost_estimate=cost(10 * rows * width, 2 * rows * width * 6),
        name="merge",
    )(h, *attn_pair, *ffn_pair, shifts, *deps)


def tn(a, b):
    return lax.dot_general(a, b, (((0,), (0,)), ((), ())), preferred_element_type=F32)


def slope_kernel(count, terms, owners_ref, *refs):
    lefts = [jnp.concatenate([ref[...] for ref in refs[t * count : (t + 1) * count]], axis=1) for t in range(terms)]
    rights = refs[terms * count : terms * (count + 1)]
    outs = refs[terms * (count + 1) :]
    share = lefts[0].shape[1] // count
    total = sum(tn(left, right[...]) for left, right in zip(lefts, rights)).astype(BF16)
    first = pl.program_id(0) < pl.num_programs(0) // 2
    for ref, here in zip(outs, (first, jnp.logical_not(first))):

        @pl.when(here)
        def _():
            for index in range(count):
                ref[index] = total[index * share : (index + 1) * share]


def slope_call(owners, terms, name, cut=(0, 1), deps=()):
    total = owners.shape[0]
    share = terms[0][0].shape[1] // total
    columns = terms[0][1].shape[1] // cut[1]
    count = 4
    if share % 128 or total % (2 * count):
        pieces = 0.0
        row = 0
        for left, right, _ in terms:
            left_ordered = jnp.take(left.reshape(left.shape[0], total, share), owners, axis=1).reshape(left.shape)
            part = right[row : row + left.shape[0], cut[0] * columns : (cut[0] + 1) * columns]
            row += left.shape[0]
            pieces = pieces + tn(left_ordered, part)
        pieces = pieces.astype(BF16).reshape(total, share, columns)
        return pieces[: total // 2], pieces[total // 2 :]
    steps = total // count
    ins, specs = [], []
    for left, _, _ in terms:
        for index in range(count):
            ins.append(left)
            specs.append(
                pl.BlockSpec((left.shape[0], share), functools.partial(lambda i, r, o: (0, o[count * r + i]), index))
            )
    for left, right, row in terms:
        ins.append(right)
        specs.append(
            pl.BlockSpec((left.shape[0], columns), functools.partial(lambda i, r, o: (i, cut[0]), row))
        )
    return pl.pallas_call(
        waiting(functools.partial(slope_kernel, count, len(terms)), 1 + len(ins), deps),
        grid_spec=pltpu.PrefetchScalarGridSpec(
            num_scalar_prefetch=1,
            grid=(steps,),
            in_specs=specs + anywhere(len(deps)),
            out_specs=halves_of(count, steps // 2, share, columns),
        ),
        out_shape=[shape_of(total // 2, share, columns)] * 2,
        compiler_params=params_of(),
        cost_estimate=cost(
            sum(2 * a.size * columns for a, _, _ in terms),
            sum(2 * (a.size + a.shape[0] * columns) for a, _, _ in terms) + 2 * total * share * columns,
        ),
        name=name,
    )(owners, *ins, *deps)


class Sums:
    def __init__(self, masks, slots, send, receive, remote, totals):
        self.masks, self.slots, self.send, self.receive = masks, slots, send, receive
        self.remote, self.totals = remote, totals
        self.steps = [0] * len(masks)
        self.running = [None] * len(masks)
        self.kept = [None] * len(masks)
        self.first = [sum(len(m) for m in masks[:c]) for c in range(len(masks))]

    def launch(self, c, kept, sent):
        step = self.steps[c]
        number = self.first[c] + step
        self.kept[c] = kept
        self.running[c] = self.remote(
            sent, self.slots[c][step], self.send.at[number], self.receive.at[number], self.masks[c][step]
        )

    def halve(self, c, pieces, count):
        self.launch(c, pieces, pieces.at[pl.ds(count // 2, count // 2)])

    def go_on(self, c):
        self.running[c].wait_recv()
        slot = self.slots[c][self.steps[c]]
        count = slot.shape[0]
        total = self.kept[c][:count].astype(F32) + slot[...].astype(F32)
        self.steps[c] += 1
        if self.steps[c] == len(self.masks[c]):
            self.totals[c](total[0])
            return
        self.kept[c][:count] = total.astype(BF16)
        self.halve(c, self.kept[c], count)


def tail_kernel(masks, *refs):
    late, early = masks
    (dq_in, dk_in, dv_in, w_in, near_in, far_in, h_in, g_in, second0_in, second1_in, gains_ref, words_in, o0_in, o1_in,
     d0_in, d1_in, ua0_in, ua1_in, ub0_in, ub1_in) = refs[:20]
    o_out, joint_out, down_out, up_out, home_ref, words_out = refs[20:26]
    (dq, dk, dv, w, near, far, h, g, second0, second1, o0, d0, d1, ua0, ua1, ub0, ub1, jq, jk, jv,
     far1, far1_got, sums, arrived, near0, near1, near1_got, d_own, words, other_words) = refs[26:56]
    slots = refs[56:74]
    load, chain_send, chain_receive, side_send, side_receive, word_send, word_receive = refs[74:]
    me, core = lax.axis_index("ctx"), lax.axis_index("tp")
    size = words.shape[0]
    rows, width = h.shape
    seqs, _, block, _ = home_ref.shape
    chips = size // seqs
    seq = me // chips
    chip_rows = 2 * rows
    other_core = {"tp": 1 - core}
    started = []

    def at_ctx(mask):
        return {"ctx": exchanged(me, mask)}

    def send(source, target, first, second, device):
        copy = pltpu.make_async_remote_copy(
            source, target, first, second, device_id=device, device_id_type=pl.DeviceIdType.MESH
        )
        copy.start()
        started.append(copy)
        return copy

    def to_core(source, target, number):
        return send(source, target, side_send.at[number], side_receive.at[number], other_core)

    loads = {}
    order = (
        ("d0", d0_in, d0), ("d1", d1_in, d1), ("ua0", ua0_in, ua0), ("ua1", ua1_in, ua1), ("ub0", ub0_in, ub0),
        ("ub1", ub1_in, ub1), ("dk", dk_in, dk), ("dv", dv_in, dv), ("w", w_in, w), ("dq", dq_in, dq), ("near", near_in, near),
        ("far", far_in, far), ("o0", o0_in, o0), ("h", h_in, h), ("g", g_in, g), ("second0", second0_in, second0),
    )
    for number, (name, source, target) in enumerate(order):
        loads[name] = pltpu.make_async_copy(source, target, load.at[number])
        loads[name].start()

    barrier = pltpu.get_barrier_semaphore()
    for mask in range(1, size):
        pl.semaphore_signal(barrier, inc=1, device_id=at_ctx(mask), device_id_type=pl.DeviceIdType.MESH)
    pl.semaphore_signal(barrier, inc=1, device_id=other_core, device_id_type=pl.DeviceIdType.MESH)
    pl.semaphore_wait(barrier, size)

    units = up_out.shape[1]

    def put_output(total):
        o_out[...] = total.T

    def put_down(total):
        down_out[...] = total.T

    def put_joint(t):
        def write(total):
            joint_out[t] = total

        return write

    def put_up(start):
        def write(total):
            up_out[:, start : start + units // 2] = total

        return write

    chains = [late, late, late, late, early[1:], early[1:], late[1:]]
    parts, used = [], 0
    for chain in chains:
        parts.append(slots[used : used + len(chain)])
        used += len(chain)
    totals = [put_output, put_joint(0), put_joint(1), put_joint(2), put_up(0), put_up(units // 2), put_down]
    run = Sums(
        chains, parts, chain_send, chain_receive,
        lambda source, target, first, second, mask: send(source, target, first, second, at_ctx(mask)), totals,
    )
    run.launch(0, o0, o1_in)
    second_swap = to_core(second1_in, second1, 0)

    def ready(c, kept, other, names):
        for name in names:
            loads[name].wait()
        for index in range(kept.shape[0]):
            kept[index] = (kept[index].astype(F32) + other[index].astype(F32)).astype(BF16)
        run.halve(c, kept, kept.shape[0])

    ready(6, d0, d1, ("d0", "d1"))
    ready(4, ua0, ua1, ("ua0", "ua1"))
    ready(5, ub0, ub1, ("ub0", "ub1"))
    for name in ("dk", "dv", "w"):
        loads[name].wait()

    def from_far(start):
        cut = slice(start, start + rows)
        return dot_nt(dk[cut], w[1]) + dot_nt(dv[cut], w[2])

    far1[...] = from_far(chip_rows + rows).astype(BF16)
    swap = to_core(far1, far1_got, 1)
    mine = from_far(chip_rows)
    swap.wait_recv()
    sums[...] = (mine + far1_got[...].astype(F32)).astype(BF16)
    arrival = send(sums, arrived, side_send.at[2], side_receive.at[2], at_ctx(1))
    loads["dq"].wait()
    loads["near"].wait()
    loads["far"].wait()
    loads["o0"].wait()

    def from_near(cut):
        return sum(dot_nt(grad[cut], w[t]) for t, grad in enumerate((dq, dk, dv)))

    near1[...] = from_near(slice(rows, chip_rows)).astype(BF16)
    near_swap = to_core(near1, near1_got, 3)
    near0[...] = from_near(slice(0, rows)).astype(BF16)
    run.go_on(0)
    share = width // size
    count = 4
    owners = mask_order(late)
    for t, (target, grad) in enumerate(((jq, dq), (jk, dk), (jv, dv))):
        for start in range(0, size, count):
            spots = [pl.ds(pl.multiple_of(exchanged(me, m) * share, share), share) for m in owners[start : start + count]]
            total = tn(jnp.concatenate([near[:, spot] for spot in spots], axis=1), grad[:chip_rows])
            if t:
                total = total + tn(jnp.concatenate([far[:, spot] for spot in spots], axis=1), grad[chip_rows:])
            low = total.astype(BF16)
            for index in range(count):
                target[start + index] = low[index * share : (index + 1) * share]
        run.halve(1 + t, target, size)
        if t == 1:
            run.go_on(6)
    for name in ("h", "g", "second0"):
        loads[name].wait()
    for copy in (second_swap, near_swap, arrival):
        copy.wait_recv()
    gradients = [jnp.zeros((1, width), F32) for _ in range(5)]
    for s in range(seqs):
        cut = slice(s * block, (s + 1) * block)
        scaled, inverse = normalize(h[cut].astype(F32))
        upstream = g[cut].astype(F32)
        d_first = near0[cut].astype(F32) + near1_got[cut].astype(F32) + arrived[cut].astype(F32)
        d_second = second0[cut].astype(F32) + second1[cut].astype(F32)
        for row, term in enumerate((d_first * scaled, d_first, d_second * scaled, d_second, upstream)):
            gradients[row] = gradients[row] + jnp.sum(term, axis=0, keepdims=True)
        d_scaled = d_first * gains_ref[0:1] + d_second * gains_ref[1:2]
        middle = jnp.mean(d_scaled, axis=-1, keepdims=True)
        along = jnp.mean(d_scaled * scaled, axis=-1, keepdims=True)
        d_own[cut] = (upstream + inverse * (d_scaled - middle - scaled * along)).astype(BF16)
    home = []
    for s in range(seqs):
        source = d_own.at[pl.ds(s * block, block)]
        if s == 0:
            stay = pltpu.make_async_copy(source, home_ref.at[seq, core], load.at[len(order)])
            stay.start()
        else:
            number = 4 + s
            home.append(
                send(source, home_ref.at[seq, core], side_send.at[number], side_receive.at[number], at_ctx(s * chips))
            )
    lines = width // 128
    words_out[...] = words_in[...]
    for row in range(5):
        for line in range(lines):
            words_out[row * lines + line : row * lines + line + 1] = gradients[row][:, line * 128 : (line + 1) * 128]
    words[pl.ds(me, 1)] = words_out[...][None]
    word_copies = [
        send(words.at[me], words.at[me], word_send.at[mask], word_receive.at[mask], at_ctx(mask))
        for mask in range(1, size)
    ]
    for c in (0, 4, 1, 2, 5, 3, 1, 6, 4, 2, 0, 5, 3):
        run.go_on(c)
    stay.wait()
    swaps = []
    for s in range(seqs):
        if s:
            home[s - 1].wait_recv()
        place = home_ref.at[exchanged(seq, s), core]
        swaps.append(to_core(place, place, 4 + seqs + s))
    for copy in word_copies:
        copy.wait_recv()
    total = words[0]
    for index in range(1, size):
        total = total + words[index]
    core_words = other_words.shape[0]
    for copy in word_copies:
        copy.wait_send()
    words_out[...] = total
    swap = to_core(words_out.at[pl.ds(0, core_words)], other_words, 4)
    swap.wait_recv()
    swap.wait_send()
    words_out[pl.ds(0, core_words)] = total[:core_words] + other_words[...]
    for c in (1, 2, 3):
        run.go_on(c)
    for copy in swaps:
        copy.wait_recv()
    for copy in started:
        if copy is not swap and not any(copy is x for x in word_copies):
            copy.wait_send()


def tail_call(grads, w_joint, normals, h, g, seconds, gains, words, core_words, output, down, ups, masks, seqs, number):
    late, early = masks
    rows, width = h.shape
    chip_rows, local = grads[0].shape
    size = 1 << len(late)
    units = down[0].shape[2]
    share = width // size
    ins = (*grads, w_joint, *normals, h, g, *seconds, gains, words, *output, *down, *ups[0], *ups[1])
    specs = anywhere(len(ins))
    specs[10], specs[11] = whole(gains.shape), whole(words.shape)
    out = [
        shape_of(local, share, dtype=F32),
        shape_of(3, share, local, dtype=F32),
        shape_of(units, share, dtype=F32),
        shape_of(share, units, dtype=F32),
        shape_of(seqs, 2, rows // seqs, width),
        shape_of(*words.shape, dtype=F32),
    ]
    half = size // 2
    wide = (rows, width)
    scratch = [x.shape for x in (*grads, w_joint, *normals)] + [wide] * 4 + [output[0].shape]
    scratch += [down[0].shape] * 2 + [ups[0][0].shape] * 4 + [(size, share, local)] * 3 + [wide] * 8
    scratch = [pltpu.VMEM(shape, BF16) for shape in scratch]
    scratch += [pltpu.VMEM((size, *words.shape), F32), pltpu.VMEM((core_words, 128), F32)]
    for chain, columns, pieces in (
        (late, local, half), (late, local, half), (late, local, half), (late, local, half),
        (early[1:], units // 2, half // 2), (early[1:], units // 2, half // 2), (late[1:], units, half // 2),
    ):
        scratch += [pltpu.VMEM((pieces >> step, share, columns), BF16) for step in range(len(chain))]
    scratch += [pltpu.SemaphoreType.DMA((17,))] + carrier_semaphores(18)
    scratch += carrier_semaphores(4 + 2 * seqs) + carrier_semaphores(size)
    return pl.pallas_call(
        functools.partial(tail_kernel, masks),
        grid=(1,),
        in_specs=specs,
        out_specs=[pl.BlockSpec(memory_space=pl.ANY) if n == 4 else whole(x.shape) for n, x in enumerate(out)],
        out_shape=out,
        scratch_shapes=scratch,
        compiler_params=params_of(collective_id=number, has_side_effects=True),
        name="tail",
    )(*ins)


def finish_kernel(chains, events, seqs, chips, core_words, *refs):
    count = len(chains)
    ins, refs = refs[: 2 * count], refs[2 * count :]
    d_own_ref, words_ref = refs[:2]
    totals, home_ref, words_out = refs[2 : 2 + count], refs[2 + count], refs[3 + count]
    refs = list(refs[4 + count :])
    current = [refs.pop(0) for _ in chains]
    slots = [[refs.pop(0) for _ in chain[0]] for chain in chains]
    words, other_words, chain_send, chain_receive, home_send, home_receive, word_send, word_receive, local = refs
    me, core = lax.axis_index("ctx"), lax.axis_index("tp")
    size = words.shape[0]
    seq = me // chips
    block = home_ref.shape[2]

    def at_ctx(mask):
        return {"ctx": exchanged(me, mask)}

    other_core = {"tp": 1 - core}

    def remote(source, target, send, receive, device):
        return pltpu.make_async_remote_copy(
            source, target, send, receive, device_id=device, device_id_type=pl.DeviceIdType.MESH
        )

    barrier = pltpu.get_barrier_semaphore()
    for mask in range(1, size):
        pl.semaphore_signal(barrier, inc=1, device_id=at_ctx(mask), device_id_type=pl.DeviceIdType.MESH)
    pl.semaphore_signal(barrier, inc=1, device_id=other_core, device_id_type=pl.DeviceIdType.MESH)
    pl.semaphore_wait(barrier, size)

    started = []

    def begin(copy):
        copy.start()
        started.append(copy)
        return copy

    word_copies = [
        begin(remote(words_ref, words.at[me], word_send.at[mask], word_receive.at[mask], at_ctx(mask)))
        for mask in range(1, size)
    ]
    steps = [0] * count
    running = [None] * count
    number = [sum(len(chain[0]) for chain in chains[:c]) for c in range(count)]

    def launch(c, source):
        masks = chains[c][0]
        step = steps[c]
        n = number[c] + step
        running[c] = begin(
            remote(source, slots[c][step], chain_send.at[n], chain_receive.at[n], at_ctx(masks[step]))
        )

    def split(c):
        pieces = current[c].shape[0] >> (steps[c] + (0 if chains[c][1] else -1))
        launch(c, current[c].at[pl.ds(pieces // 2, pieces // 2)])

    home = []

    def send_home():
        copy = pltpu.make_async_copy(d_own_ref.at[pl.ds(0, block)], home_ref.at[seq, core], local)
        copy.start()
        for s in range(1, seqs):
            home.append(
                begin(
                    remote(
                        d_own_ref.at[pl.ds(s * block, block)], home_ref.at[seq, core],
                        home_send.at[s], home_receive.at[s], at_ctx(s * chips),
                    )
                )
            )
        copy.wait()

    def go_on(c):
        masks, ready = chains[c][:2]
        running[c].wait_recv()
        slot = slots[c][steps[c]]
        pieces = slot.shape[0]
        kept = ins[2 * c] if steps[c] == 0 and not ready else current[c]
        total = kept[:pieces].astype(F32) + slot[...].astype(F32)
        steps[c] += 1
        if steps[c] == len(masks):
            totals[c][...] = total[0]
            return
        current[c][:pieces] = total.astype(BF16)
        split(c)

    for c, (masks, ready, _) in enumerate(chains):
        if not ready:
            launch(c, ins[2 * c + 1])
    for c, (masks, ready, _) in enumerate(chains):
        if ready:
            current[c][...] = (ins[2 * c][...].astype(F32) + ins[2 * c + 1][...].astype(F32)).astype(BF16)
            split(c)
    send_home()
    words[pl.ds(me, 1)] = words_ref[...][None]
    for c in events:
        go_on(c)
    for copy in home:
        copy.wait_recv()
    swaps = []
    for s in range(seqs):
        place = home_ref.at[exchanged(seq, s), core]
        swaps.append(begin(remote(place, place, home_send.at[seqs + s], home_receive.at[seqs + s], other_core)))
    for copy in word_copies:
        copy.wait_recv()
    total = words[0]
    for index in range(1, size):
        total = total + words[index]
    words_out[...] = total
    swap = remote(words_out.at[pl.ds(0, core_words)], other_words, word_send.at[0], word_receive.at[0], other_core)
    swap.start()
    swap.wait()
    words_out[pl.ds(0, core_words)] = total[:core_words] + other_words[...]
    for copy in swaps:
        copy.wait_recv()
    for copy in started:
        copy.wait_send()


def finish_call(chains, events, d_own, words, core_words, seqs, chips, number):
    size = chips * seqs
    rows, width = d_own.shape
    block = rows // seqs
    ins, specs, out, scratch, slots = [], [], [], [], []
    for masks, ready, (kept, other) in chains:
        pieces, share, columns = kept.shape
        ins += [kept, other]
        specs += [whole(kept.shape), whole(other.shape) if ready else anywhere(1)[0]]
        out.append(shape_of(share, columns, dtype=F32))
        scratch.append(pltpu.VMEM((pieces, share, columns), BF16))
        slots += [
            pltpu.VMEM((pieces >> (step + 1 if ready else step), share, columns), BF16) for step in range(len(masks))
        ]
    copies = len(slots)
    scratch += slots + [pltpu.VMEM((size, *words.shape), F32), pltpu.VMEM((core_words, 128), F32)]
    scratch += carrier_semaphores(copies) + carrier_semaphores(2 * seqs) + carrier_semaphores(size)
    scratch += [pltpu.SemaphoreType.DMA]
    home = shape_of(seqs, 2, block, width)
    out_specs = [whole(x.shape) for x in out] + anywhere(1) + [whole(words.shape)]
    return pl.pallas_call(
        functools.partial(finish_kernel, [(m, r, None) for m, r, _ in chains], events, seqs, chips, core_words),
        grid=(1,),
        in_specs=specs + anywhere(1) + [whole(words.shape)],
        out_specs=out_specs,
        out_shape=out + [home, shape_of(*words.shape, dtype=F32)],
        scratch_shapes=scratch,
        compiler_params=params_of(collective_id=number, has_side_effects=True),
        name="finish",
    )(*ins, d_own, words)


def swap_core(shard):
    return lax.ppermute(shard, "tp", [(0, 1), (1, 0)])


def swap_ctx(shard, mask):
    return lax.ppermute(shard, "ctx", [(c, c ^ mask) for c in range(lax.axis_size("ctx"))])


def next_section(shard, by):
    size = lax.axis_size("section")
    return lax.ppermute(shard, "section", [(s, s + by) for s in range(size) if 0 <= s + by < size])


def mask_order(masks):
    order = [0]
    for mask in reversed(masks):
        order = order + [value ^ mask for value in order]
    return order


def on_device(
    tokens,
    cotangent,
    block_order,
    first_gain,
    first_bias,
    second_gain,
    second_bias,
    joint_weight,
    joint_bias,
    output_weight,
    output_bias,
    up_weight,
    up_bias,
    down_weight,
    down_bias,
):
    section = lax.axis_index("section")
    sections = lax.axis_size("section")
    ctx = lax.axis_index("ctx")
    ctx_size = lax.axis_size("ctx")
    core = lax.axis_index("tp")
    seqs, local_len, width = tokens.shape
    block = local_len // 2
    chips = ctx_size // seqs
    seq, member = ctx // chips, ctx % chips
    rows = seqs * block
    chip_rows = 2 * rows
    length = chips * chip_rows
    seq_masks = [chips << b for b in range((seqs - 1).bit_length())]
    member_masks = [1 << b for b in range((chips - 1).bit_length())]

    k, u, a = jnp.meshgrid(jnp.arange(chips), jnp.arange(2), jnp.arange(seqs), indexing="ij")
    stored = (2 * ((seq ^ a) * chips + (member ^ k)) + (core ^ u)).reshape(-1)
    places = block_order[stored]
    spots = (places[:, None] * block + jnp.arange(block, dtype=jnp.int32)).reshape(-1)
    exponent = jnp.arange(ROT // 2, dtype=F32) * (2.0 / ROT)
    inverse = jnp.power(jnp.float32(ROTARY_BASE), -exponent)
    turns = spots.astype(F32)[:, None] * inverse[None, :]
    cosine, sine = jnp.cos(turns), jnp.sin(turns)
    rest = jnp.zeros((length, HEAD - ROT), F32)
    table = (
        jnp.tile(jnp.concatenate([cosine, cosine, rest + 1.0], 1), (1, 128 // HEAD)),
        jnp.tile(jnp.concatenate([sine, sine, rest], 1), (1, 128 // HEAD)),
    )

    tile = max(block, 128)
    tile_places = places[: chip_rows // block].reshape(-1, tile // block)
    lowest, highest = jnp.min(tile_places, 1), jnp.max(tile_places, 1)
    limits = jnp.stack([(lowest * block + 1) // KEY_TILE, (highest * block + block - 1) // KEY_TILE + 1], 1)

    gain_one, shift_one, gain_two, shift_two = first_gain, first_bias, second_gain, second_bias
    w_joint, b_joint = joint_weight[0], joint_bias[0]
    w_output, b_output = output_weight[0], output_bias
    w_up, b_up = up_weight[0], up_bias
    w_down, b_down = down_weight[0], down_bias
    gains = jnp.concatenate([gain_one, gain_two], 0)
    norms = jnp.concatenate([gain_one, shift_one, gain_two, shift_two], 0)
    shifts = jnp.concatenate([b_output, b_down], 0)

    def plane_parts(values):
        mine = lax.dynamic_slice_in_dim(values, core * block, block, 1)
        return [lax.dynamic_index_in_dim(mine, seq ^ shift, 0, keepdims=False) for shift in range(seqs)]

    def from_planes(values):
        parts = values.reshape(seqs, block, width)
        return [parts[s] if s == 0 else swap_ctx(parts[s], s * chips) for s in range(seqs)]

    def in_order(parts):
        parts = jnp.stack(parts)
        both = jnp.stack([parts, swap_core(parts)], 1)
        ordered = [
            lax.dynamic_index_in_dim(lax.dynamic_index_in_dim(both, s ^ seq, 0, False), v ^ core, 0, False)
            for s in range(seqs)
            for v in range(2)
        ]
        return jnp.stack(ordered).reshape(1, seqs, local_len, width)

    def paired(parts):
        count = len(parts) // 2
        return tuple(x[0] if count == 1 else jnp.concatenate(x, 0) for x in (parts[:count], parts[count:]))

    def forward(own, save, moves, moved, name, number):
        chip = (own, swap_core(own))
        moves = [("ctx", k) for k in range(1, chips)] + moves
        outs, arrived = front_call(
            chip, norms, w_joint, b_joint, table, w_up, b_up, w_down, save, moves, [own] * (chips - 1) + moved, name, number
        )
        normal, keys, values, queries, ffn0, ffn1, *kept_ffn = outs
        others, arrived = arrived[: chips - 1], arrived[chips - 1 :]
        key_parts, value_parts, normal_parts = [keys], [values], [normal]
        if chips > 1:
            rest = paired([x for other in others for x in (other, swap_core(other))])
            far_normal, far_keys, far_values = joint_call(
                rest, gain_one, shift_one, w_joint, b_joint, table, chip_rows
            )
            key_parts.append(far_keys)
            value_parts.append(far_values)
            normal_parts.append(far_normal)
        attn0, attn1, mixture, lse = attend_call(queries, key_parts, value_parts, places, limits, w_output, block)
        result, moments = merge_call(own, (attn0, swap_core(attn1)), (ffn0, swap_core(ffn1)), shifts)
        return result, moments, (normal_parts, queries, key_parts, value_parts, mixture, lse, *kept_ffn), arrived

    def attention_back(g_pair, kept, deps=()):
        normal_parts, queries, key_parts, value_parts, mixture, lse, second_in, active, slope = kept
        return attend_back_call(
            queries, g_pair, mixture, lse, key_parts, value_parts, places, limits, w_output, table, block, deps
        )

    def far_back(d_keys, d_values, deps=()):
        if chips == 1:
            return []
        far = joint_back_call([d_keys, d_values], chip_rows, length - chip_rows, w_joint, deps)
        if chips > 2:
            far = jnp.concatenate(far, 0).reshape(chips - 1, 2, rows, width)
            far = far[:, 0], far[:, 1]
        sums = (far[0].astype(F32) + swap_core(far[1]).astype(F32)).astype(BF16).reshape(chips - 1, rows, width)
        return [sums[k - 1] for k in range(1, chips)]

    others = [("ctx", k) for k in range(1, chips)]
    planes = [("ctx", s * chips) for s in range(1, seqs)]
    token_parts = plane_parts(tokens)
    token_rows = jnp.concatenate([token_parts[0]] + [swap_ctx(token_parts[s], s * chips) for s in range(1, seqs)], 0)
    g_parts = plane_parts(cotangent)
    own = token_rows
    for tick in range(sections):
        first = tick == 0
        result, moments, kept, arrived = forward(
            own, tick == sections - 1, planes if first else [], g_parts[1:] if first else [], "front" + str(tick), tick
        )
        if first:
            g_rows = jnp.concatenate([g_parts[0], *arrived], 0)
        if tick < sections - 1:
            own = jnp.where(section == 0, token_rows, next_section(result, 1))
    out_parts = from_planes(result)
    moments = jnp.sum(moments[:3], axis=1)
    normal_parts, queries, key_parts, value_parts, mixture, lse, second_in, active, slope = kept
    g_own = g_rows
    for tick in range(sections - 1):
        g_pair = (g_own, swap_core(g_own))
        d_queries, d_keys, d_values, _ = attention_back(g_pair, kept)
        sums = far_back(d_keys, d_values, tuple(out_parts) if tick == 0 else ())
        near, second, arrivals = rear_call(
            (d_queries, d_keys, d_values), w_joint, g_pair, slope, w_up, w_down, others, sums, "rear" + str(tick), sections + tick
        )
        firsts = [near[0], swap_core(near[1]), *arrivals]
        d_own, _ = norm_back_call(own, g_own, firsts, [second[0], swap_core(second[1])], gains)
        g_own = jnp.where(section == sections - 1, g_rows, next_section(d_own, -1))
    section_out = in_order(out_parts)

    local = w_output.shape[0]
    units = w_up.shape[1]

    def results(section_out, home, small, core_words, joint_total, output_total, up_total, down_total):
        both, ones = small[:core_words].reshape(-1), small[core_words:].reshape(-1)
        norm_total = both[: 5 * width].reshape(5, 1, width)
        root_means = jnp.sqrt(both[5 * width : 5 * width + 3] / (length * seqs * width))
        return (
            section_out,
            home.reshape(1, seqs, local_len, width),
            norm_total[0],
            norm_total[1],
            norm_total[2],
            norm_total[3],
            joint_total[None],
            ones[: 3 * local].reshape(1, 3, local),
            output_total[None],
            norm_total[4],
            up_total[None],
            ones[3 * local : 3 * local + units].reshape(1, units),
            down_total[None],
            norm_total[4],
            root_means[None],
        )

    late = tuple(member_masks + seq_masks)
    early = tuple(seq_masks + member_masks)
    late_owners = jnp.stack([ctx ^ m for m in mask_order(late)]).astype(jnp.int32)
    early_owners = jnp.stack([ctx ^ m for m in mask_order(early)]).astype(jnp.int32)
    share = width // ctx_size
    g_pair = (g_own, swap_core(g_own))
    by_blocks = share % 128 == 0 and chips == 2

    def of_g(right, name, deps=()):
        if by_blocks:
            terms = [(g_pair[0], right, 0), (g_pair[1], right, 1)]
        else:
            terms = [(jnp.concatenate(g_pair, 0), right, 0)]
        return slope_call(late_owners, terms, name, (0, 1), deps)

    down = of_g(active, "down_slope")
    down_arrived = swap_ctx(down[1], late[0])
    output = of_g(mixture, "output_slope", (down[0],))
    second0, second1, d_hidden, up_sums = ffn_back_call(g_pair, slope, w_up, w_down, (output[0],))
    ups = [slope_call(early_owners, [(second_in, d_hidden, 0)], "up_slope", (0, 2))]
    ups.append(slope_call(early_owners, [(second_in, d_hidden, 0)], "up_slope", (1, 2), (ups[0][0],)))
    ups_arrived = [swap_ctx(part[1], early[0]) for part in ups]
    d_queries, d_keys, d_values, joint_sums = attention_back(g_pair, kept, (ups[1][0], output[0]))
    seconds = [second0, second1]

    def in_words(values):
        values = values.reshape(-1)
        return jnp.pad(values, (0, -values.size % 1024)).reshape(-1, 128)

    grads = (d_queries, d_keys, d_values)
    ones = in_words(jnp.concatenate([joint_sums[:3].reshape(-1), up_sums.reshape(-1)]))
    if by_blocks and len(late) == 3:
        both = in_words(jnp.concatenate([jnp.zeros((5 * width,), F32), moments]))
        pairs = [(part[0], there) for part, there in zip(ups, ups_arrived)]
        output_total, joint_total, down_total, up_total, home, small = tail_call(
            grads, w_joint, normal_parts, own, g_own, seconds, gains, jnp.concatenate([both, ones], 0), both.shape[0],
            output, (down[0], down_arrived), pairs, (late, early), seqs, 2 * sections,
        )
        return results(section_out, home, small, both.shape[0], joint_total, output_total, up_total, down_total)
    sums = far_back(d_keys, d_values, (down_arrived, *ups_arrived))

    def halved(pair, arrived):
        total = (pair[0].astype(F32) + arrived.astype(F32)).astype(BF16)
        return total[: total.shape[0] // 2], total[total.shape[0] // 2 :]

    down = halved(down, down_arrived)
    ups[0] = halved(ups[0], ups_arrived[0])
    near = joint_back_call(grads, 0, chip_rows, w_joint)
    down_arrived, ups_arrived[0] = swap_ctx(down[1], late[1]), swap_ctx(ups[0][1], early[1])
    arrivals = [swap_ctx(part, k + 1) for k, part in enumerate(sums)]
    joints = [slope_call(late_owners, [(normal_parts[0], d_queries, 0)], "query_slope")]
    for grad in grads[1:]:
        joints.append(slope_call(late_owners, [(part, grad, n) for n, part in enumerate(normal_parts)], "key_slope"))
    firsts = [near[0], swap_core(near[1]), *arrivals]
    d_own, norm_sums = norm_back_call(own, g_own, firsts, [second0, swap_core(second1)], gains)
    both = in_words(jnp.concatenate([norm_sums[:5].reshape(-1), moments]))
    chains = [
        (late, False, output),
        (late, False, joints[0]),
        (late, False, joints[1]),
        (late, False, joints[2]),
        (early[1:], True, (ups[1][0], ups_arrived[1])),
        (late[2:], True, (down[0], down_arrived)),
        (early[2:], True, (ups[0][0], ups_arrived[0])),
    ]
    events = [c for step in range(len(late)) for c, chain in enumerate(chains) if step < len(chain[0])]
    output_total, *joint_total, up_right, down_total, up_left, home, small = finish_call(
        chains, events, d_own, jnp.concatenate([both, ones], 0), both.shape[0], seqs, chips, 2 * sections + 1
    )
    joint_total = jnp.stack(joint_total)
    up_total = jnp.concatenate([up_left, up_right], 1)
    output_total, down_total = output_total.T, down_total.T
    return results(section_out, home, small, both.shape[0], joint_total, output_total, up_total, down_total)


def solution(mesh):
    in_specs = (
        P(None, "ctx", None),
        P(None, "ctx", None),
        P(),
        P("section", None),
        P("section", None),
        P("section", None),
        P("section", None),
        P("section", None, None, "tp"),
        P("section", None, "tp"),
        P("section", "tp", None),
        P("section", None),
        P("section", None, "tp"),
        P("section", "tp"),
        P("section", "tp", None),
        P("section", None),
    )
    out_specs = (
        P("section", None, "ctx", None),
        P("section", None, "ctx", None),
        P("section", None),
        P("section", None),
        P("section", None),
        P("section", None),
        P("section", None, "ctx", "tp"),
        P("section", None, "tp"),
        P("section", "tp", "ctx"),
        P("section", None),
        P("section", "ctx", "tp"),
        P("section", "tp"),
        P("section", "tp", "ctx"),
        P("section", None),
        P("section", None),
    )
    return jax.shard_map(
        on_device, mesh=mesh, in_specs=in_specs, out_specs=out_specs, check_vma=False
    )
```

profile of v0, /device:TPU:0, one launch (start us, length us, event | category | flops | bytes accessed | tf_op | source)
XLA Modules:
  0.0 631.3 jit_solution(7690581402846186176)
XLA Ops:
  2.2 3.1 collective-permute-start
  5.3 2.6 collective-permute-start.1
  9.2 7.2 %collective-permute-done = bf16[128,1024]{1,0:T(8,128)(2,1)S(1)} collective-permute-done((bf16[128,1024]{1,0:T(8,128)(2,1)S(1)}, bf16[128,1024]{1,0:T(8,128)(2,1)S(1)}, u32[]{:S(2)}, u32[]{:S(2)}) %collective-permute-start) | collective-permute-done | bytes 262176 | tf_op jit(solution)/shard_map/ppermute | solution.py:1154
  16.4 10.3 %collective-permute-done.1 = bf16[128,1024]{1,0:T(8,128)(2,1)S(1)} collective-permute-done((bf16[128,1024]{1,0:T(8,128)(2,1)S(1)}, bf16[128,1024]{1,0:T(8,128)(2,1)S(1)}, u32[]{:S(2)}, u32[]{:S(2)}) %collective-permute-start.1) | collective-permute-done | bytes 262176 | tf_op jit(solution)/shard_map/ppermute | solution.py:1154
  33.5 38.6 %front0.1 = (bf16[1024,1024]{1,0:T(8,128)(2,1)}, bf16[1024,512]{1,0:T(8,128)(2,1)}, bf16[1024,512]{1,0:T(8,128)(2,1)}, bf16[1024,512]{1,0:T(8,128)(2,1)}, bf16[5...) custom-call(bf16[512,1024]{1,0:T(8,128)(2,1)} %copy-done.5, ...), custom_call_target="tpu_custom_call" | custom-call | flops 11811160064 | bytes 16777216 | tf_op jit(solution)/shard_map/front0/pallas_call | solution.py:224
  76.0 7.5 %joint_projection.2 = (bf16[1024,1024]{1,0:T(8,128)(2,1)}, bf16[1024,512]{1,0:T(8,128)(2,1)}, bf16[1024,512]{1,0:T(8,128)(2,1)}) custom-call(bf16[512,1024]{1,0:T(8,128)(2,1)} %get-tuple-element.83.refs_0_, bf16[512,1024]{1,0:T(8,128)(2,1)} %copy-done.42, f32[1,1024]{1,0:T(1,128)} %refs_2_.3, f32[1,1024]{1,0:T(1,128)} %refs_3_.3, ...), custom_call_target="tpu_custom_call" | custom-call | flops 2147483648 | bytes 7340032 | tf_op jit(solution)/shard_map/joint_projection/pallas_call | solution.py:162
  83.5 24.3 %attend.2 = (bf16[512,1024]{1,0:T(8,128)(2,1)}, bf16[512,1024]{1,0:T(8,128)(2,1)}, bf16[1024,512]{1,0:T(8,128)(2,1)}, f32[8,2,512]{2,1,0:T(2,128)}) custom-call(s32[16]{0:T(128)} %copy-done.41, s32[8,2]{1,0:T(8,128)} %copy.52.refs_1_, bf16[1024,512]{1,0:T(8,128)(2,1)} %get-tuple-element.81.refs_2_, bf16[512,1024]{1,0:T(8,128)(2,1)} %bitcast.124, ...), custom_call_target="tpu_custom_call" | custom-call | flops 12884901888 | bytes 8388608 | tf_op jit(solution)/shard_map/attend/pallas_call | solution.py:383
  111.8 4.6 merge.2
  116.4 3.4 collective-permute-start.7
  119.8 22.9 %collective-permute-done.7 = bf16[512,1024]{1,0:T(8,128)(2,1)S(1)} collective-permute-done((bf16[512,1024]{1,0:T(8,128)(2,1)}, bf16[512,1024]{1,0:T(8,128)(2,1)S(1)}, u32[]{:S(2)}, u32[]{:S(2)}) %collective-permute-start.7) | collective-permute-done | bytes 1048608 | tf_op jit(solution)/shard_map/ppermute | solution.py:1159
  143.3 2.6 collective-permute-done.8.refs_1_
  146.9 36.8 %front1.1 = (bf16[1024,1024]{1,0:T(8,128)(2,1)}, bf16[1024,512]{1,0:T(8,128)(2,1)}, bf16[1024,512]{1,0:T(8,128)(2,1)}, bf16[1024,512]{1,0:T(8,128)(2,1)}, bf16[5...) custom-call(bf16[512,1024]{1,0:T(8,128)(2,1)} %copy-done.4, ...), custom_call_target="tpu_custom_call" | custom-call | flops 11811160064 | bytes 16777216 | tf_op jit(solution)/shard_map/front1/pallas_call | solution.py:224
  184.3 2.4 collective-permute-done.9.refs_1_
  187.7 7.5 %joint_projection.3 = (bf16[1024,1024]{1,0:T(8,128)(2,1)}, bf16[1024,512]{1,0:T(8,128)(2,1)}, bf16[1024,512]{1,0:T(8,128)(2,1)}) custom-call(bf16[512,1024]{1,0:T(8,128)(2,1)} %get-tuple-element.94.refs_0_, bf16[512,1024]{1,0:T(8,128)(2,1)} %copy-done.44, f32[1,1024]{1,0:T(1,128)} %refs_2_.3, f32[1,1024]{1,0:T(1,128)} %refs_3_.3, ...), custom_call_target="tpu_custom_call" | custom-call | flops 2147483648 | bytes 7340032 | tf_op jit(solution)/shard_map/joint_projection/pallas_call | solution.py:162
  195.2 24.4 %attend.3 = (bf16[512,1024]{1,0:T(8,128)(2,1)}, bf16[512,1024]{1,0:T(8,128)(2,1)}, bf16[1024,512]{1,0:T(8,128)(2,1)}, f32[8,2,512]{2,1,0:T(2,128)}) custom-call(s32[16]{0:T(128)} %copy-done.41, s32[8,2]{1,0:T(8,128)} %copy.52.refs_1_, bf16[1024,512]{1,0:T(8,128)(2,1)} %get-tuple-element.92.refs_2_, bf16[512,1024]{1,0:T(8,128)(2,1)} %bitcast.125, ...), custom_call_target="tpu_custom_call" | custom-call | flops 12884901888 | bytes 8388608 | tf_op jit(solution)/shard_map/attend/pallas_call | solution.py:383
  223.6 4.9 merge.3
  232.6 2.4 collective-permute-start.14
  235.0 46.3 %attend_back.2 = (bf16[1024,512]{1,0:T(8,128)(2,1)}, bf16[2048,512]{1,0:T(8,128)(2,1)}, bf16[2048,512]{1,0:T(8,128)(2,1)}, f32[8,512]{1,0:T(8,128)}) custom-call(s32[16]{0:T(128)} %copy-done.41, s32[8,2]{1,0:T(8,128)} %copy.52.refs_1_, bf16[1024,512]{1,0:T(8,128)(2,1)} %get-tuple-element.92.refs_2_, bf16[512,1024]{1,0:T(8,128)(2,1)} %copy-done.6, ...), custom_call_target="tpu_custom_call" | custom-call | flops 25769803776 | bytes 16777216 | tf_op jit(solution)/shard_map/attend_back/pallas_call | solution.py:496
  282.1 6.3 %joint_projection_back.1 = (bf16[512,1024]{1,0:T(8,128)(2,1)}, bf16[512,1024]{1,0:T(8,128)(2,1)}) custom-call(bf16[2048,512]{1,0:T(8,128)(2,1)} %get-tuple-element.109.refs_0_.refs_1_, bf16[2048,512]{1,0:T(8,128)(2,1)} %get-tuple-element.110.refs_1_.refs_2_, bf16[3,1024,512]{2,1,0:T(8,128)(2,1)} %bitcast.90, bf16[128,1024]{1,0:T(8,128)(2,1)} %get-tuple-element.200.refs_3_, ...), custom_call_target="tpu_custom_call" | custom-call | flops 2147483648 | bytes 8388608 | tf_op jit(solution)/shard_map/joint_projection_back/pallas_call | solution.py:539
  288.5 2.9 collective-permute-done.17
  291.3 2.5 add_convert_fusion.refs_9_
  293.9 43.6 %rear0.1 = (bf16[512,1024]{1,0:T(8,128)(2,1)}, bf16[512,1024]{1,0:T(8,128)(2,1)}, bf16[512,1024]{1,0:T(8,128)(2,1)}, bf16[512,1024]{1,0:T(8,128)(2,1)}, bf16[512,1024]{1,0:T(8,128)(2,1)}) custom-call(bf16[1024,512]{1,0:T(8,128)(2,1)} %get-tuple-element.108.refs_0_, bf16[2048,512]{1,0:T(8,128)(2,1)} %get-tuple-element.109.refs_0_.refs_1_, ...), custom_call_target="tpu_custom_call" | custom-call | flops 11811160064 | bytes 16777216 | tf_op jit(solution)/shard_map/rear0/pallas_call | solution.py:573
  343.0 6.2 norm_back.1
  353.4 23.2 %collective-permute-done.20 = bf16[512,1024]{1,0:T(8,128)(2,1)S(1)} collective-permute-done((bf16[512,1024]{1,0:T(8,128)(2,1)}, bf16[512,1024]{1,0:T(8,128)(2,1)S(1)}, u32[]{:S(2)}, u32[]{:S(2)}) %collective-permute-start.20) | collective-permute-done | bytes 1048608 | tf_op jit(solution)/shard_map/ppermute | solution.py:1159
  385.4 11.0 %down_slope.1 = (bf16[4,128,2048]{2,1,0:T(8,128)(2,1)}, bf16[4,128,2048]{2,1,0:T(8,128)(2,1)}) custom-call(s32[8]{0:T(128)} %stack.93.refs_0_, bf16[512,1024]{1,0:T(8,128)(2,1)} %copy-done.2, bf16[512,1024]{1,0:T(8,128)(2,1)} %copy-done.2, bf16[512,1024]{1,0:T(8,128)(2,1)} %copy-done.2, bf16[512,1024]{1,0:T(8,128)(2,1)} %copy-done.2, ...), custom_call_target="tpu_custom_call" | custom-call | flops 4294967296 | bytes 10485760 | tf_op jit(solution)/shard_map/down_slope/pallas_call | solution.py:702
  396.4 5.3 output_slope.1
  401.7 16.6 %feed_forward_back.1 = (bf16[512,1024]{1,0:T(8,128)(2,1)}, bf16[512,1024]{1,0:T(8,128)(2,1)}, bf16[1024,2048]{1,0:T(8,128)(2,1)}, f32[1,2048]{1,0:T(1,128)}) custom-call(bf16[512,1024]{1,0:T(8,128)(2,1)} %copy-done.2, bf16[512,1024]{1,0:T(8,128)(2,1)} %copy-done.3, bf16[1024,2048]{1,0:T(8,128)(2,1)} %get-tuple-element.111.refs_6_.refs_2_, ...), custom_call_target="tpu_custom_call" | custom-call | flops 8589934592 | bytes 20971520 | tf_op jit(solution)/shard_map/feed_forward_back/pallas_call | solution.py:262
  418.3 6.9 %up_slope.2 = (bf16[4,128,1024]{2,1,0:T(8,128)(2,1)}, bf16[4,128,1024]{2,1,0:T(8,128)(2,1)}) custom-call(s32[8]{0:T(128)} %stack.92.refs_0_, bf16[1024,1024]{1,0:T(8,128)(2,1)} %get-tuple-element.120.refs_1_.refs_2_.refs_3_.refs_4_, bf16[1024,1024]{1,0:T(8,128)(2,1)} %get-tuple-element.120.refs_1_.refs_2_.refs_3_.refs_4_, ...), custom_call_target="tpu_custom_call" | custom-call | flops 2147483648 | bytes 6291456 | tf_op jit(solution)/shard_map/up_slope/pallas_call | solution.py:702
  425.2 6.9 %up_slope.3 = (bf16[4,128,1024]{2,1,0:T(8,128)(2,1)}, bf16[4,128,1024]{2,1,0:T(8,128)(2,1)}) custom-call(s32[8]{0:T(128)} %stack.92.refs_0_, bf16[1024,1024]{1,0:T(8,128)(2,1)} %get-tuple-element.120.refs_1_.refs_2_.refs_3_.refs_4_, bf16[1024,1024]{1,0:T(8,128)(2,1)} %get-tuple-element.120.refs_1_.refs_2_.refs_3_.refs_4_, ...), custom_call_target="tpu_custom_call" | custom-call | flops 2147483648 | bytes 6291456 | tf_op jit(solution)/shard_map/up_slope/pallas_call | solution.py:702
  435.9 46.4 %attend_back.3 = (bf16[1024,512]{1,0:T(8,128)(2,1)}, bf16[2048,512]{1,0:T(8,128)(2,1)}, bf16[2048,512]{1,0:T(8,128)(2,1)}, f32[8,512]{1,0:T(8,128)}) custom-call(s32[16]{0:T(128)} %copy-done.41, s32[8,2]{1,0:T(8,128)} %copy.52.refs_1_, bf16[1024,512]{1,0:T(8,128)(2,1)} %get-tuple-element.92.refs_2_, bf16[512,1024]{1,0:T(8,128)(2,1)} %copy-done.2, ...), custom_call_target="tpu_custom_call" | custom-call | flops 25769803776 | bytes 16777216 | tf_op jit(solution)/shard_map/attend_back/pallas_call | solution.py:496
  485.4 132.9 %tail.1 = (f32[512,128]{1,0:T(8,128)}, f32[3,128,512]{2,1,0:T(8,128)}, f32[2048,128]{1,0:T(8,128)}, f32[128,2048]{1,0:T(8,128)}, bf16[4,2,128,1024]{3,2,1,0:T(8,128)(2,1)}, /*index=5*/f32[80,128]{1,0:T(8,128)}) custom-call(bf16[1024,512]{1,0:T(8,128)(2,1)} %get-tuple-element.127.refs_0_, bf16[2048,512]{1,0:T(8,128)(2,1)} %get-tuple-element.128.refs_1_, ...), custom_call_target="tpu_custom_call" | custom-call | tf_op jit(solution)/shard_map/tail/pallas_call | solution.py:985
  624.1 3.2 copy.82
  (192 shorter events, 63.7 us)
Async XLA Ops:
  2.2 14.2 %collective-permute-start = (bf16[128,1024]{1,0:T(8,128)(2,1)S(1)}, bf16[128,1024]{1,0:T(8,128)(2,1)S(1)}, u32[]{:S(2)}, u32[]{:S(2)}) collective-permute-start(bf16[128,1024]{1,0:T(8,128)(2,1)S(1)} %get-tuple-element.197), channel_id=1, source_target_pairs={{0,4},{2,6},{4,0},{6,2},{8,12},{10,14},{12,8},{14,10},{1,5},{3,7},... | collective-permute-start | bytes 786440 | tf_op jit(solution)/shard_map/ppermute | solution.py:1154
  5.3 21.4 %collective-permute-start.1 = (bf16[128,1024]{1,0:T(8,128)(2,1)S(1)}, bf16[128,1024]{1,0:T(8,128)(2,1)S(1)}, u32[]{:S(2)}, u32[]{:S(2)}) collective-permute-start(bf16[128,1024]{1,0:T(8,128)(2,1)S(1)} %get-tuple-element.199), channel_id=1, source_target_pairs={{0,8},{2,10},{4,12},{6,14},{8,0},{10,2},{12,4},{14,6},{1,9},{3,11}... | collective-permute-start | bytes 786440 | tf_op jit(solution)/shard_map/ppermute | solution.py:1154
  7.9 18.8 %collective-permute-start.2 = (bf16[128,1024]{1,0:T(8,128)(2,1)S(1)}, bf16[128,1024]{1,0:T(8,128)(2,1)S(1)}, u32[]{:S(2)}, u32[]{:S(2)}) collective-permute-start(bf16[128,1024]{1,0:T(8,128)(2,1)S(1)} %get-tuple-element.198), channel_id=1, source_target_pairs={{0,12},{2,14},{4,8},{6,10},{8,4},{10,6},{12,0},{14,2},{1,13},{3,15... | collective-permute-start | bytes 786440 | tf_op jit(solution)/shard_map/ppermute | solution.py:1154
  8.7 63.4 %copy-start.41 = (s32[16]{0:T(128)}, s32[16]{0:T(128)S(1)}, u32[]{:S(2)}) copy-start(s32[16]{0:T(128)S(1)} %gather_fusion) | copy-start | bytes 196
  26.7 6.7 %collective-permute-start.3 = (bf16[512,1024]{1,0:T(8,128)(2,1)S(1)}, bf16[512,1024]{1,0:T(8,128)(2,1)}, u32[]{:S(2)}, u32[]{:S(2)}) collective-permute-start(bf16[512,1024]{1,0:T(8,128)(2,1)S(1)} %pad_maximum_fusion.refs_0_.refs_10_), channel_id=1, source_target_pairs={{0,1},{1,0},{2,3},{3,2},{4,5},{5,4},{6,7},{7,6},{8,9},{9,8},{10,11... | collective-permute-start | bytes 3145736 | tf_op jit(solution)/shard_map/ppermute | solution.py:1150
  72.0 2.9 collective-permute-start.4
  72.8 35.8 %collective-permute-start.6 = (bf16[512,1024]{1,0:T(8,128)(2,1)}, bf16[512,1024]{1,0:T(8,128)(2,1)S(1)}, u32[]{:S(2)}, u32[]{:S(2)}) collective-permute-start(bf16[512,1024]{1,0:T(8,128)(2,1)} %get-tuple-element.90), channel_id=1, source_target_pairs={{0,1},{1,0},{2,3},{3,2},{4,5},{5,4},{6,7},{7,6},{8,9},{9,8},{10,11... | collective-permute-start | bytes 3145736 | tf_op jit(solution)/shard_map/ppermute | solution.py:1150
  107.9 2.9 collective-permute-start.5
  116.4 26.4 %collective-permute-start.7 = (bf16[512,1024]{1,0:T(8,128)(2,1)}, bf16[512,1024]{1,0:T(8,128)(2,1)S(1)}, u32[]{:S(2)}, u32[]{:S(2)}) collective-permute-start(bf16[512,1024]{1,0:T(8,128)(2,1)} %get-tuple-element.91), channel_id=1, source_target_pairs={{0,16},{1,17},{2,18},{3,19},{4,20},{5,21},{6,22},{7,23},{8,24},{9,... | collective-permute-start | bytes 3145736 | tf_op jit(solution)/shard_map/ppermute | solution.py:1159
  143.2 2.7 collective-permute-start.8
  183.8 2.9 collective-permute-start.9
  183.8 37.5 %collective-permute-start.11 = (bf16[512,1024]{1,0:T(8,128)(2,1)}, bf16[512,1024]{1,0:T(8,128)(2,1)S(1)}, u32[]{:S(2)}, u32[]{:S(2)}) collective-permute-start(bf16[512,1024]{1,0:T(8,128)(2,1)} %get-tuple-element.101), channel_id=1, source_target_pairs={{0,1},{1,0},{2,3},{3,2},{4,5},{5,4},{6,7},{7,6},{8,9},{9,8},{10,11... | collective-permute-start | bytes 3145736 | tf_op jit(solution)/shard_map/ppermute | solution.py:1150
  195.2 24.6 %copy-start.23 = (bf16[128,1024]{1,0:T(8,128)(2,1)S(1)}, bf16[128,1024]{1,0:T(8,128)(2,1)}, u32[]{:S(2)}) copy-start(bf16[128,1024]{1,0:T(8,128)(2,1)} %get-tuple-element.103) | copy-start | bytes 786436
  195.2 24.6 %copy-start.25 = (bf16[128,1024]{1,0:T(8,128)(2,1)S(1)}, bf16[128,1024]{1,0:T(8,128)(2,1)}, u32[]{:S(2)}) copy-start(bf16[128,1024]{1,0:T(8,128)(2,1)} %get-tuple-element.104) | copy-start | bytes 786436
  219.6 2.9 collective-permute-start.10
  220.9 14.1 %collective-permute-start.16 = (bf16[512,1024]{1,0:T(8,128)(2,1)S(1)}, bf16[512,1024]{1,0:T(8,128)(2,1)}, u32[]{:S(2)}, u32[]{:S(2)}) collective-permute-start(bf16[512,1024]{1,0:T(8,128)(2,1)S(1)} %pad_maximum_fusion.2.refs_3_.refs_4_.refs_1_), channel_id=1, source_target_pairs={{0,1},{1,0},{2,3},{3,2},{4,5},{5,4},{6,7},{7,6},{8,9},{9,8},{10,11... | collective-permute-start | bytes 3145736 | tf_op jit(solution)/shard_map/ppermute | solution.py:1150
  230.6 50.7 %collective-permute-start.12 = (bf16[128,1024]{1,0:T(8,128)(2,1)S(1)}, bf16[128,1024]{1,0:T(8,128)(2,1)S(1)}, u32[]{:S(2)}, u32[]{:S(2)}) collective-permute-start(bf16[128,1024]{1,0:T(8,128)(2,1)S(1)} %get-tuple-element.204), channel_id=1, source_target_pairs={{0,4},{2,6},{4,0},{6,2},{8,12},{10,14},{12,8},{14,10},{1,5},{3,7},... | collective-permute-start | bytes 786440 | tf_op jit(solution)/shard_map/ppermute | solution.py:1154
  231.2 50.1 %collective-permute-start.13 = (bf16[128,1024]{1,0:T(8,128)(2,1)S(1)}, bf16[128,1024]{1,0:T(8,128)(2,1)S(1)}, u32[]{:S(2)}, u32[]{:S(2)}) collective-permute-start(bf16[128,1024]{1,0:T(8,128)(2,1)S(1)} %get-tuple-element.203), channel_id=1, source_target_pairs={{0,8},{2,10},{4,12},{6,14},{8,0},{10,2},{12,4},{14,6},{1,9},{3,11}... | collective-permute-start | bytes 786440 | tf_op jit(solution)/shard_map/ppermute | solution.py:1154
  232.6 48.7 %collective-permute-start.14 = (bf16[128,1024]{1,0:T(8,128)(2,1)S(1)}, bf16[128,1024]{1,0:T(8,128)(2,1)S(1)}, u32[]{:S(2)}, u32[]{:S(2)}) collective-permute-start(bf16[128,1024]{1,0:T(8,128)(2,1)S(1)} %get-tuple-element.202), channel_id=1, source_target_pairs={{0,12},{2,14},{4,8},{6,10},{8,4},{10,6},{12,0},{14,2},{1,13},{3,15... | collective-permute-start | bytes 786440 | tf_op jit(solution)/shard_map/ppermute | solution.py:1154
  288.5 2.9 collective-permute-start.17
  293.9 44.2 %copy-start.33 = (f32[1,1024]{1,0:T(1,128)S(1)}, f32[1,1024]{1,0:T(1,128)}, u32[]{:S(2)}) copy-start(f32[1,1024]{1,0:T(1,128)} %refs_2_.3) | copy-start | bytes 12292
  337.5 2.9 collective-permute-start.18
  337.6 4.4 collective-permute-start.19
  349.2 27.5 %copy-start.24 = (bf16[128,1024]{1,0:T(8,128)(2,1)S(1)}, bf16[128,1024]{1,0:T(8,128)(2,1)}, u32[]{:S(2)}) copy-start(bf16[128,1024]{1,0:T(8,128)(2,1)} %get-tuple-element.103) | copy-start | bytes 786436
  349.2 27.5 %copy-start.26 = (bf16[128,1024]{1,0:T(8,128)(2,1)S(1)}, bf16[128,1024]{1,0:T(8,128)(2,1)}, u32[]{:S(2)}) copy-start(bf16[128,1024]{1,0:T(8,128)(2,1)} %get-tuple-element.104) | copy-start | bytes 786436
  349.2 27.4 %collective-permute-start.20 = (bf16[512,1024]{1,0:T(8,128)(2,1)}, bf16[512,1024]{1,0:T(8,128)(2,1)S(1)}, u32[]{:S(2)}, u32[]{:S(2)}) collective-permute-start(bf16[512,1024]{1,0:T(8,128)(2,1)} %get-tuple-element.119), channel_id=1, source_target_pairs={{16,0},{17,1},{18,2},{19,3},{20,4},{21,5},{22,6},{23,7},{24,8},{25... | collective-permute-start | bytes 3145736 | tf_op jit(solution)/shard_map/ppermute | solution.py:1159
  351.8 26.3 %collective-permute-start.15 = (bf16[4,128,1024]{2,1,0:T(8,128)(2,1)}, bf16[4,128,1024]{2,1,0:T(8,128)(2,1)}, u32[]{:S(2)}, u32[]{:S(2)}) collective-permute-start(bf16[4,128,1024]{2,1,0:T(8,128)(2,1)} %get-tuple-element.206), channel_id=1, source_target_pairs={{0,1},{1,0},{2,3},{3,2},{4,5},{5,4},{6,7},{7,6},{8,9},{9,8},{10,11... | collective-permute-start | bytes 3145736 | tf_op jit(solution)/shard_map/ppermute | solution.py:1150
  378.1 5.0 collective-permute-start.21
  432.1 51.5 %collective-permute-start.24 = (bf16[4,128,1024]{2,1,0:T(8,128)(2,1)}, bf16[4,128,1024]{2,1,0:T(8,128)(2,1)S(1)}, u32[]{:S(2)}, u32[]{:S(2)}) collective-permute-start(bf16[4,128,1024]{2,1,0:T(8,128)(2,1)} %get-tuple-element.140), channel_id=1, source_target_pairs={{0,4},{2,6},{4,0},{6,2},{8,12},{10,14},{12,8},{14,10},{1,5},{3,7},... | collective-permute-start | bytes 3145736 | tf_op jit(solution)/shard_map/ppermute | solution.py:1154
  432.1 51.5 %collective-permute-start.23 = (bf16[4,128,1024]{2,1,0:T(8,128)(2,1)}, bf16[4,128,1024]{2,1,0:T(8,128)(2,1)}, u32[]{:S(2)}, u32[]{:S(2)}) collective-permute-start(bf16[4,128,1024]{2,1,0:T(8,128)(2,1)} %get-tuple-element.139), channel_id=1, source_target_pairs={{0,4},{2,6},{4,0},{6,2},{8,12},{10,14},{12,8},{14,10},{1,5},{3,7},... | collective-permute-start | bytes 3145736 | tf_op jit(solution)/shard_map/ppermute | solution.py:1154
  434.2 49.5 %collective-permute-start.22 = (bf16[4,128,2048]{2,1,0:T(8,128)(2,1)}, bf16[4,128,2048]{2,1,0:T(8,128)(2,1)S(1)}, u32[]{:S(2)}, u32[]{:S(2)}) collective-permute-start(bf16[4,128,2048]{2,1,0:T(8,128)(2,1)} %get-tuple-element.138), channel_id=1, source_target_pairs={{0,2},{2,0},{4,6},{6,4},{8,10},{10,8},{12,14},{14,12},{1,3},{3,1},... | collective-permute-start | bytes 6291464 | tf_op jit(solution)/shard_map/ppermute | solution.py:1154
  435.9 47.1 %copy-start.35 = (f32[1,2048]{1,0:T(1,128)S(1)}, f32[1,2048]{1,0:T(1,128)}, u32[]{:S(2)}) copy-start(f32[1,2048]{1,0:T(1,128)} %get-tuple-element.136) | copy-start | bytes 24580
  (38 other events, 149.7 us)
where the time goes:
time: 638 us; the launch traced here: 631 us
  Pallas kernels  477 us (75%)
  waiting for transfers between devices  79.8 us (13%)
  local copies, waits for them, and re-layouts  35.7 us (6%)
  starting transfers between devices  21.6 us (3%)
  other arithmetic  15.3 us (2%)
    pallas_call x1, Pallas kernels, tail_call(): pl.pallas_call(functools.partial(tail_kernel, masks), grid=(1,), in_specs...  133 us
    pallas_call x2, Pallas kernels, attend_back_call(): pl.pallas_call(waiting(functools.partial(attend_back_kernel, block, tile,...  92.6 us
    pallas_call x2, Pallas kernels, front_call(): pl.pallas_call(carrying(functools.partial(front_kernel, save), 2 + len(in...  75.4 us
    pallas_call x2, Pallas kernels, attend_call(): pl.pallas_call(waiting(functools.partial(attend_kernel, block, tile, len(...  48.7 us
    ppermute x2, waiting for transfers between devices, next_section(): lax.ppermute(shard, 'section', [(s, s + by) for s in range(size) if 0 <=...  46.2 us
    pallas_call x1, Pallas kernels, rear_call(): pl.pallas_call(carrying(rear_kernel, 9, 4, moves), grid=(2 * rows // tile...  43.6 us
    pallas_call x4, Pallas kernels, slope_call(): pl.pallas_call(waiting(functools.partial(slope_kernel, count, len(terms))...  30.1 us
    unnamed x97, local copies, waits for them, and re-layouts  18.8 us
  transfers between devices with their start and end apart: 25, of which 12 were waited for; matrix products, arithmetic and copies ran while one was open for 4% of the time, Pallas kernels for 26%

commit v1 on v0

--- a/solution.py
+++ b/solution.py
@@ -12,6 +12,7 @@
 EPS = 1e-05
 ROTARY_BASE = 10000.0
 NEGATIVE = -1e30
+SEQS = 4
 STACK = 4
 GROUP = STACK * HEAD
 KEY_TILE = 512
@@ -233,6 +234,246 @@
         name=name,
     )(*pair, *ins, *moved)
     return outs[: len(out)], outs[len(out) :]
+
+
+class Traffic:
+    def __init__(self):
+        self.started = []
+
+    def send(self, source, target, first, second, device):
+        copy = pltpu.make_async_remote_copy(
+            source, target, first, second, device_id=device, device_id_type=pl.DeviceIdType.MESH
+        )
+        copy.start()
+        self.started.append(copy)
+        return copy
+
+    def finish(self):
+        for copy in self.started:
+            copy.wait_send()
+
+
+def greet(partners):
+    barrier = pltpu.get_barrier_semaphore()
+    for partner in partners:
+        pl.semaphore_signal(barrier, inc=1, device_id=partner, device_id_type=pl.DeviceIdType.MESH)
+    pl.semaphore_wait(barrier, len(partners))
+
+
+def gather_kernel(first, save, seqs, *refs):
+    refs = list(refs)
+    take = lambda count: [refs.pop(0) for _ in range(count)]
+    norms_ref, b_joint_ref, cos_ref, sin_ref, up_b_ref, w_in, up_in, down_in = take(8)
+    if first:
+        tokens_ref, cotangent_ref = take(2)
+    else:
+        shifts_ref, a0_in, a1_in, f0_in, f1_in, h_in = take(6)
+    outs = take(13 if save else 10)
+    own_out, far_outs, near_outs = outs[0], outs[1:4], outs[4:]
+    if first:
+        g_out = take(1)[0]
+    own, other, far0, far1, w, up, down = take(7)
+    far_stage = take(3)
+    near_stage = take(len(near_outs))
+    if not first:
+        a0, a1, f0, f1, h, got, a_got, f_got = take(8)
+    load, store, arrive_s, arrive_r, core_s, core_r, chip_s, chip_r, far_s, far_r, side_s, side_r = refs
+    me, core, section = lax.axis_index("ctx"), lax.axis_index("tp"), lax.axis_index("section")
+    rows, width = own.shape
+    block = rows // seqs
+    chips = 2
+    seq = me // chips
+    other_core, other_chip, twin = {"tp": 1 - core}, {"ctx": exchanged(me, 1)}, {"section": 1 - section}
+    traffic = Traffic()
+
+    def at(c):
+        return pl.ds(c * block, block)
+
+    copies = [pltpu.make_async_copy(a, b, load.at[n]) for n, (a, b) in enumerate(((w_in, w), (up_in, up), (down_in, down)))]
+    if not first:
+        extra = [
+            pltpu.make_async_copy(a, b, load.at[3 + n])
+            for n, (a, b) in enumerate(((a0_in, a0), (f0_in, f0), (h_in, h)))
+        ]
+        for copy in extra:
+            copy.start()
+    for copy in copies:
+        copy.start()
+    if first:
+        planes = [{"ctx": exchanged(me, c * chips)} for c in range(1, seqs)]
+        greet([other_core, other_chip] + planes)
+        mine = pl.ds(pl.multiple_of(core * block, block), block)
+        stay = [
+            pltpu.make_async_copy(tokens_ref.at[seq, mine], own.at[at(0)], load.at[3]),
+            pltpu.make_async_copy(cotangent_ref.at[seq, mine], g_out.at[at(0)], load.at[4]),
+        ]
+        for copy in stay:
+            copy.start()
+        arrivals = [None]
+        for c in range(1, seqs):
+            source = tokens_ref.at[exchanged(seq, c), mine]
+            arrivals.append(traffic.send(source, own.at[at(c)], arrive_s.at[c], arrive_r.at[c], planes[c - 1]))
+        sides = []
+        for c in range(1, seqs):
+            source = cotangent_ref.at[exchanged(seq, c), mine]
+            sides.append(traffic.send(source, g_out.at[at(c)], side_s.at[c], side_r.at[c], planes[c - 1]))
+    else:
+        greet([other_core, other_chip, twin])
+        swaps = [
+            traffic.send(a1_in, a_got, side_s.at[0], side_r.at[0], other_core),
+            traffic.send(f1_in, f_got, side_s.at[1], side_r.at[1], other_core),
+        ]
+        for copy in extra:
+            copy.wait()
+        for copy in swaps:
+            copy.wait_recv()
+        arrivals = []
+        for c in range(seqs):
+            cut = slice(c * block, (c + 1) * block)
+            attention = a0[cut].astype(F32) + a_got[cut].astype(F32) + shifts_ref[0:1]
+            feedforward = f0[cut].astype(F32) + f_got[cut].astype(F32) + shifts_ref[1:2]
+            a1[cut] = (h[cut].astype(F32) + attention + feedforward).astype(BF16)
+            arrivals.append(traffic.send(a1.at[at(c)], got.at[at(c)], arrive_s.at[c], arrive_r.at[c], twin))
+
+    to_core, to_chip, to_far = [None] * seqs, [None] * seqs, [None] * seqs
+
+    def arrive(c):
+        if first and c == 0:
+            stay[0].wait()
+        else:
+            arrivals[c].wait_recv()
+        if not first:
+            cut = slice(c * block, (c + 1) * block)
+            own[cut] = jnp.where(section == 0, h[cut], got[cut])
+        here = own.at[at(c)]
+        to_core[c] = traffic.send(here, other.at[at(c)], core_s.at[c], core_r.at[c], other_core)
+        to_chip[c] = traffic.send(here, far0.at[at(c)], chip_s.at[c], chip_r.at[c], other_chip)
+
+    def arrive_far(c):
+        to_chip[c].wait_recv()
+        to_far[c] = traffic.send(far0.at[at(c)], far1.at[at(c)], far_s.at[c], far_r.at[c], other_core)
+
+    n_st, k_st, v_st, q_st, part0_st, part1_st = near_stage[:6]
+    half = rows // 2
+
+    def near_rows(ref, part, value, base=0):
+        ref[base + part * half : base + (part + 1) * half] = value
+
+    def near_joint(part):
+        cut = slice(part * half, (part + 1) * half)
+        scaled, _ = normalize(jnp.concatenate([own[cut], other[cut]], 0).astype(F32))
+        low = (scaled * norms_ref[0:1] + norms_ref[1:2]).astype(BF16)
+        second = (scaled * norms_ref[2:3] + norms_ref[3:4]).astype(BF16)
+        turns = [
+            jnp.concatenate([ref[cut], ref[rows + part * half : rows + (part + 1) * half]], 0) for ref in (cos_ref, sin_ref)
+        ]
+        queries = turn(dot(low, w[0]) + b_joint_ref[0:1], *turns) * HEAD ** (-0.5)
+        keys = turn(dot(low, w[1]) + b_joint_ref[1:2], *turns)
+        values = dot(low, w[2]) + b_joint_ref[2:3]
+        for ref, value in ((n_st, low), (q_st, queries), (k_st, keys), (v_st, values)):
+            value = value.astype(BF16)
+            near_rows(ref, part, value[:half])
+            near_rows(ref, part, value[half:], rows)
+        if save:
+            near_rows(near_stage[6], part, second[:half])
+            near_rows(near_stage[6], part, second[half:], rows)
+        return second
+
+    def near_ffn(part, low):
+        total = None
+        for start in range(0, up.shape[1], 512):
+            cut = slice(start, start + 512)
+            hidden = dot(low, up[:, cut]) + up_b_ref[:, cut]
+            share, bell = gelu_parts(hidden)
+            active = (hidden * share).astype(BF16)
+            if save:
+                slope = (share + hidden * bell * 0.3989422804014327).astype(BF16)
+                for ref, value in ((near_stage[7], active), (near_stage[8], slope)):
+                    ref[part * half : (part + 1) * half, cut] = value[:half]
+                    ref[rows + part * half : rows + (part + 1) * half, cut] = value[half:]
+            term = dot(active, down[cut, :])
+            total = term if total is None else total + term
+        near_rows(part0_st, part, total[:half].astype(BF16))
+        near_rows(part1_st, part, total[half:].astype(BF16))
+
+    def far_joint(u, ref):
+        scaled, _ = normalize(ref[...].astype(F32))
+        low = (scaled * norms_ref[0:1] + norms_ref[1:2]).astype(BF16)
+        cut = slice(u * rows, (u + 1) * rows)
+        turns = [table[2 * rows + u * rows : 2 * rows + (u + 1) * rows] for table in (cos_ref, sin_ref)]
+        far_stage[0][cut] = low
+        far_stage[1][cut] = turn(dot(low, w[1]) + b_joint_ref[1:2], *turns).astype(BF16)
+        far_stage[2][cut] = (dot(low, w[2]) + b_joint_ref[2:3]).astype(BF16)
+
+    arrive(0)
+    arrive(1)
+    copies[0].wait()
+    for c in (0, 1):
+        to_core[c].wait_recv()
+    low = near_joint(0)
+    if not first:
+        arrive(2)
+    copies[1].wait()
+    copies[2].wait()
+    near_ffn(0, low)
+    if first:
+        arrive(2)
+    arrive(3)
+    arrive_far(0)
+    arrive_far(1)
+    for c in (2, 3):
+        to_core[c].wait_recv()
+    low = near_joint(1)
+    arrive_far(2)
+    near_ffn(1, low)
+    arrive_far(3)
+    stores = [pltpu.make_async_copy(own, own_out, store.at[0])]
+    stores += [pltpu.make_async_copy(a, b, store.at[1 + n]) for n, (a, b) in enumerate(zip(near_stage, near_outs))]
+    for copy in stores:
+        copy.start()
+    far_joint(0, far0)
+    for c in range(seqs):
+        to_far[c].wait_recv()
+    far_joint(1, far1)
+    base = 1 + len(near_outs)
+    late = [pltpu.make_async_copy(a, b, store.at[base + n]) for n, (a, b) in enumerate(zip(far_stage, far_outs))]
+    for copy in late:
+        copy.start()
+    if first:
+        stay[1].wait()
+        for copy in sides:
+            copy.wait_recv()
+    traffic.finish()
+    for copy in stores + late:
+        copy.wait()
+
+
+def gather_call(first, save, norms, w_joint, b_joint, table, w_up, b_up, w_down, sources, name, number):
+    rows = (sources[0].shape[0] * sources[0].shape[1] // 2) if first else sources[-1].shape[0]
+    seqs = SEQS
+    width, local, units = w_up.shape[0], w_joint.shape[2], w_up.shape[1]
+    wide, narrow = (rows, width), (2 * rows, local)
+    near = [(2 * rows, width), narrow, narrow, narrow, wide, wide]
+    if save:
+        near += [(2 * rows, width), (2 * rows, units), (2 * rows, units)]
+    far = [(2 * rows, width), narrow, narrow]
+    out = [wide, *far, *near] + ([wide] if first else [])
+    ins = (norms, b_joint, *table, b_up)
+    extra = [] if first else [whole(sources[0].shape)]
+    scratch = [wide] * 4 + [w_joint.shape, w_up.shape, w_down.shape] + far + near + ([] if first else [wide] * 8)
+    pair = carrier_semaphores(seqs)
+    return pl.pallas_call(
+        functools.partial(gather_kernel, first, save, seqs),
+        grid=(1,),
+        in_specs=[whole(x.shape) for x in ins] + anywhere(3) + extra + anywhere(len(sources) - len(extra)),
+        out_specs=anywhere(len(out)),
+        out_shape=[shape_of(*x) for x in out],
+        scratch_shapes=[pltpu.VMEM(x, BF16) for x in scratch]
+        + [pltpu.SemaphoreType.DMA((6,)), pltpu.SemaphoreType.DMA((len(out),))]
+        + pair * 5,
+        compiler_params=params_of(collective_id=number, has_side_effects=True),
+        name=name,
+    )(*ins, w_joint, w_up, w_down, *sources)
 
 
 def ffn_back_kernel(g0_ref, g1_ref, slope_ref, up_ref, down_ref, part0_ref, part1_ref, hidden_ref, sums_ref):
@@ -715,6 +956,156 @@
         ),
         name=name,
     )(owners, *ins, *deps)
+
+
+def hand_back_kernel(seqs, *refs):
+    refs = list(refs)
+    take = lambda count: [refs.pop(0) for _ in range(count)]
+    gains_ref, shifts_ref = take(2)
+    sources = take(12)
+    a1_in, f1_in = take(2)
+    g0_out, g1_out, home_ref, moments_ref = take(4)
+    targets = take(12)
+    dk, dv, w, dq, g1, g0, down, up, slope, a0, f0, h = targets
+    far1, far1_got, sums, arrived, near0, near1, near1_got = take(7)
+    second0, second1, second1_got, d_own, got, fresh, fresh_other, a_got, f_got, result = take(10)
+    load, side_s, side_r, chip_s, chip_r, core_s, core_r, twin_s, twin_r, new_s, new_r, home_s, home_r, swap_s, swap_r = refs
+    me, core, section = lax.axis_index("ctx"), lax.axis_index("tp"), lax.axis_index("section")
+    rows, width = far1.shape
+    block = rows // seqs
+    chips = 2
+    seq = me // chips
+    chip_rows = 2 * rows
+    other_core, other_chip, twin = {"tp": 1 - core}, {"ctx": exchanged(me, 1)}, {"section": 1 - section}
+    planes = [{"ctx": exchanged(me, c * chips)} for c in range(1, seqs)]
+    traffic = Traffic()
+
+    def at(c):
+        return pl.ds(c * block, block)
+
+    def span(c):
+        return slice(c * block, (c + 1) * block)
+
+    loads = [pltpu.make_async_copy(a, b, load.at[n]) for n, (a, b) in enumerate(zip(sources, targets))]
+    for copy in loads:
+        copy.start()
+    greet([other_core, other_chip, twin] + planes)
+    out_swaps = [
+        traffic.send(a1_in, a_got, side_s.at[0], side_r.at[0], other_core),
+        traffic.send(f1_in, f_got, side_s.at[1], side_r.at[1], other_core),
+    ]
+    for n in (0, 1, 2):
+        loads[n].wait()
+
+    def from_far(start):
+        cut = slice(start, start + rows)
+        return dot_nt(dk[cut], w[1]) + dot_nt(dv[cut], w[2])
+
+    far1[...] = from_far(chip_rows + rows).astype(BF16)
+    swap = traffic.send(far1, far1_got, side_s.at[2], side_r.at[2], other_core)
+    mine = from_far(chip_rows)
+    swap.wait_recv()
+    sums[...] = (mine + far1_got[...].astype(F32)).astype(BF16)
+    arrivals = [
+        traffic.send(sums.at[at(c)], arrived.at[at(c)], chip_s.at[c], chip_r.at[c], other_chip) for c in range(seqs)
+    ]
+    for n in range(3, 12):
+        loads[n].wait()
+
+    def from_near(cut):
+        return sum(dot_nt(grad[cut], w[t]) for t, grad in enumerate((dq, dk, dv)))
+
+    near1[...] = from_near(slice(rows, chip_rows)).astype(BF16)
+    near_swap = traffic.send(near1, near1_got, side_s.at[3], side_r.at[3], other_core)
+    near0[...] = from_near(slice(0, rows)).astype(BF16)
+    for copy in out_swaps:
+        copy.wait_recv()
+    moments_ref[...] = jnp.zeros_like(moments_ref)
+    home = []
+    for c in range(seqs):
+        cut = span(c)
+        state = h[cut].astype(F32)
+        attention = a0[cut].astype(F32) + a_got[cut].astype(F32) + shifts_ref[0:1]
+        feedforward = f0[cut].astype(F32) + f_got[cut].astype(F32) + shifts_ref[1:2]
+        result[cut] = (state + attention + feedforward).astype(BF16)
+        for row, term in enumerate((state, attention, feedforward)):
+            moments_ref[row : row + 1, :] += jnp.sum(term * term, axis=0, keepdims=True)
+        place = home_ref.at[seq, core]
+        if c == 0:
+            stay = pltpu.make_async_copy(result.at[at(0)], place, load.at[12])
+            stay.start()
+        else:
+            home.append(traffic.send(result.at[at(c)], place, home_s.at[c], home_r.at[c], planes[c - 1]))
+    near_swap.wait_recv()
+    handed = []
+    for c in range(seqs):
+        cut = span(c)
+        upstream = jnp.concatenate([g0[cut], g1[cut]], 0)
+        slopes = [slice(part * rows + c * block, part * rows + (c + 1) * block) for part in range(2)]
+        total = None
+        for start in range(0, up.shape[1], 512):
+            unit = slice(start, start + 512)
+            d_active = dot_nt(upstream, down[unit, :])
+            bend = jnp.concatenate([slope[rows_cut, unit] for rows_cut in slopes], 0).astype(F32)
+            term = dot_nt((d_active * bend).astype(BF16), up[:, unit])
+            total = term if total is None else total + term
+        second1[cut] = total[block:].astype(BF16)
+        swap = traffic.send(second1.at[at(c)], second1_got.at[at(c)], core_s.at[c], core_r.at[c], other_core)
+        arrivals[c].wait_recv()
+        scaled, inverse = normalize(h[cut].astype(F32))
+        d_first = near0[cut].astype(F32) + near1_got[cut].astype(F32) + arrived[cut].astype(F32)
+        swap.wait_recv()
+        d_second = total[:block] + second1_got[cut].astype(F32)
+        d_scaled = d_first * gains_ref[0:1] + d_second * gains_ref[1:2]
+        middle = jnp.mean(d_scaled, axis=-1, keepdims=True)
+        along = jnp.mean(d_scaled * scaled, axis=-1, keepdims=True)
+        d_own[cut] = (g0[cut].astype(F32) + inverse * (d_scaled - middle - scaled * along)).astype(BF16)
+        handed.append(traffic.send(d_own.at[at(c)], got.at[at(c)], twin_s.at[c], twin_r.at[c], twin))
+    stay.wait()
+    swaps = []
+    for s in range(seqs):
+        if s:
+            home[s - 1].wait_recv()
+        place = home_ref.at[exchanged(seq, s), core]
+        swaps.append(traffic.send(place, place, swap_s.at[s], swap_r.at[s], other_core))
+    news = []
+    for c in range(seqs):
+        handed[c].wait_recv()
+        cut = span(c)
+        fresh[cut] = jnp.where(section == 1, g0[cut], got[cut])
+        news.append(traffic.send(fresh.at[at(c)], fresh_other.at[at(c)], new_s.at[c], new_r.at[c], other_core))
+    first = pltpu.make_async_copy(fresh, g0_out, load.at[0])
+    first.start()
+    for copy in news:
+        copy.wait_recv()
+    last = pltpu.make_async_copy(fresh_other, g1_out, load.at[1])
+    last.start()
+    for copy in swaps:
+        copy.wait_recv()
+    traffic.finish()
+    first.wait()
+    last.wait()
+
+
+def hand_back_call(grads, w_joint, h, g_pair, slope, w_up, w_down, gains, shifts, attn, ffn, name, number):
+    d_queries, d_keys, d_values = grads
+    rows, width = h.shape
+    seqs = SEQS
+    wide = (rows, width)
+    sources = (d_keys, d_values, w_joint, d_queries, g_pair[1], g_pair[0], w_down, w_up, slope, attn[0], ffn[0], h)
+    home = (seqs, 2, rows // seqs, width)
+    scratch = [x.shape for x in sources] + [wide] * 17
+    quads = carrier_semaphores(seqs)
+    return pl.pallas_call(
+        functools.partial(hand_back_kernel, seqs),
+        grid=(1,),
+        in_specs=[whole(gains.shape), whole(shifts.shape)] + anywhere(14),
+        out_specs=anywhere(3) + [whole((8, width))],
+        out_shape=[shape_of(*wide), shape_of(*wide), shape_of(*home), shape_of(8, width, dtype=F32)],
+        scratch_shapes=[pltpu.VMEM(x, BF16) for x in scratch] + [pltpu.SemaphoreType.DMA((14,))] + quads * 7,
+        compiler_params=params_of(collective_id=number, has_side_effects=True),
+        name=name,
+    )(gains, shifts, *sources, attn[1], ffn[1])
 
 
 class Sums:
@@ -1287,34 +1678,61 @@
 
     others = [("ctx", k) for k in range(1, chips)]
     planes = [("ctx", s * chips) for s in range(1, seqs)]
-    token_parts = plane_parts(tokens)
-    token_rows = jnp.concatenate([token_parts[0]] + [swap_ctx(token_parts[s], s * chips) for s in range(1, seqs)], 0)
-    g_parts = plane_parts(cotangent)
-    own = token_rows
-    for tick in range(sections):
-        first = tick == 0
-        result, moments, kept, arrived = forward(
-            own, tick == sections - 1, planes if first else [], g_parts[1:] if first else [], "front" + str(tick), tick
+    fused = chips == 2 and sections == 2 and seqs == SEQS and block % 128 == 0
+    if fused:
+        weights = (norms, w_joint, b_joint, table, w_up, b_up, w_down)
+        token_rows, *kept, g_rows = gather_call(True, False, *weights, (tokens, cotangent), "gather0", 0)
+        attn0, attn1, _, _ = attend_call(
+            kept[6], [kept[4], kept[1]], [kept[5], kept[2]], places, limits, w_output, block
         )
-        if first:
-            g_rows = jnp.concatenate([g_parts[0], *arrived], 0)
-        if tick < sections - 1:
-            own = jnp.where(section == 0, token_rows, next_section(result, 1))
-    out_parts = from_planes(result)
-    moments = jnp.sum(moments[:3], axis=1)
+        own, *kept = gather_call(
+            False, True, *weights, (shifts, attn0, attn1, kept[7], kept[8], token_rows), "gather1", 1
+        )
+        far_normal, far_keys, far_values, normal, keys, values, queries, ffn0, ffn1, *kept_ffn = kept
+        key_parts, value_parts, normal_parts = [keys, far_keys], [values, far_values], [normal, far_normal]
+        attn0, attn1, mixture, lse = attend_call(queries, key_parts, value_parts, places, limits, w_output, block)
+        kept = (normal_parts, queries, key_parts, value_parts, mixture, lse, *kept_ffn)
+        slope = kept_ffn[2]
+        g_pair = (g_rows, swap_core(g_rows))
+        d_queries, d_keys, d_values, _ = attention_back(g_pair, kept)
+        g_own, g_other, home, moments = hand_back_call(
+            (d_queries, d_keys, d_values), w_joint, own, g_pair, slope, w_up, w_down, gains, shifts,
+            (attn0, attn1), (ffn0, ffn1), "hand_back", 2,
+        )
+        section_out = home.reshape(1, seqs, local_len, width)
+        moments = jnp.sum(moments[:3], axis=1)
+        g_pair = (g_own, g_other)
+    else:
+        token_parts = plane_parts(tokens)
+        token_rows = jnp.concatenate([token_parts[0]] + [swap_ctx(token_parts[s], s * chips) for s in range(1, seqs)], 0)
+        g_parts = plane_parts(cotangent)
+        own = token_rows
+        for tick in range(sections):
+            first = tick == 0
+            result, moments, kept, arrived = forward(
+                own, tick == sections - 1, planes if first else [], g_parts[1:] if first else [], "front" + str(tick), tick
+            )
+            if first:
+                g_rows = jnp.concatenate([g_parts[0], *arrived], 0)
+            if tick < sections - 1:
+                own = jnp.where(section == 0, token_rows, next_section(result, 1))
+        out_parts = from_planes(result)
+        moments = jnp.sum(moments[:3], axis=1)
+        slope = kept[-1]
+        g_own = g_rows
+        for tick in range(sections - 1):
+            g_pair = (g_own, swap_core(g_own))
+            d_queries, d_keys, d_values, _ = attention_back(g_pair, kept)
+            sums = far_back(d_keys, d_values, tuple(out_parts) if tick == 0 else ())
+            near, second, arrivals = rear_call(
+                (d_queries, d_keys, d_values), w_joint, g_pair, slope, w_up, w_down, others, sums, "rear" + str(tick), sections + tick
+            )
+            firsts = [near[0], swap_core(near[1]), *arrivals]
+            d_own, _ = norm_back_call(own, g_own, firsts, [second[0], swap_core(second[1])], gains)
+            g_own = jnp.where(section == sections - 1, g_rows, next_section(d_own, -1))
+        section_out = in_order(out_parts)
+        g_pair = (g_own, swap_core(g_own))
     normal_parts, queries, key_parts, value_parts, mixture, lse, second_in, active, slope = kept
-    g_own = g_rows
-    for tick in range(sections - 1):
-        g_pair = (g_own, swap_core(g_own))
-        d_queries, d_keys, d_values, _ = attention_back(g_pair, kept)
-        sums = far_back(d_keys, d_values, tuple(out_parts) if tick == 0 else ())
-        near, second, arrivals = rear_call(
-            (d_queries, d_keys, d_values), w_joint, g_pair, slope, w_up, w_down, others, sums, "rear" + str(tick), sections + tick
-        )
-        firsts = [near[0], swap_core(near[1]), *arrivals]
-        d_own, _ = norm_back_call(own, g_own, firsts, [second[0], swap_core(second[1])], gains)
-        g_own = jnp.where(section == sections - 1, g_rows, next_section(d_own, -1))
-    section_out = in_order(out_parts)
 
     local = w_output.shape[0]
     units = w_up.shape[1]
@@ -1346,7 +1764,6 @@
     late_owners = jnp.stack([ctx ^ m for m in mask_order(late)]).astype(jnp.int32)
     early_owners = jnp.stack([ctx ^ m for m in mask_order(early)]).astype(jnp.int32)
     share = width // ctx_size
-    g_pair = (g_own, swap_core(g_own))
     by_blocks = share % 128 == 0 and chips == 2
 
     def of_g(right, name, deps=()):

time: 638 us -> 524 us (0.82)
  waiting for transfers between devices: 79.8 us -> 0.01 us
  starting transfers between devices: 21.6 us -> 4.39 us
  local copies, waits for them, and re-layouts: 35.7 us -> 22.8 us
  other arithmetic: 15.3 us -> 3.24 us
  Pallas kernels: 477 us -> 486 us
    ppermute x2 -> x0, waiting for transfers between devices: 46.2 us -> none  [next_section(): lax.ppermute(shard, 'section', [(s, s + by) for s in range(size) if 0 <=...]
    ppermute x9 -> x3, waiting for transfers between devices: 17.4 us -> 0.01 us  [swap_ctx(): lax.ppermute(shard, 'ctx', [(c, c ^ mask) for c in range(lax.axis_size('c...]
    ppermute x14 -> x1, waiting for transfers between devices: 16.1 us -> 0.01 us  [swap_core(): return lax.ppermute(shard, 'tp', [(0, 1), (1, 0)])]
    ppermute x9 -> x3, starting transfers between devices: 13.9 us -> 4.32 us  [swap_ctx(): lax.ppermute(shard, 'ctx', [(c, c ^ mask) for c in range(lax.axis_size('c...]
    unnamed x97 -> x52, local copies, waits for them, and re-layouts: 18.8 us -> 11.8 us
    pallas_call x9 -> x3, Pallas kernels: 156 us -> 163 us  [the longest x2 102 us: gather_call(): pl.pallas_call(functools.partial(gather_kernel, first, save, seqs), grid=...]
  transfers between devices with their start and end apart: 25 -> 4, of which waited for: 12 -> 0; matrix products, arithmetic and copies ran while one was open for 4% -> 1% of each run, Pallas kernels for 26% -> 29%
where the time goes in v1:
time: 524 us; the launch traced here: 517 us
  Pallas kernels  486 us (93%)
  local copies, waits for them, and re-layouts  22.8 us (4%)
    pallas_call x1, Pallas kernels, tail_call(): pl.pallas_call(functools.partial(tail_kernel, masks), grid=(1,), in_specs...  135 us
    pallas_call x2, Pallas kernels, gather_call(): pl.pallas_call(functools.partial(gather_kernel, first, save, seqs), grid=...  102 us
    pallas_call x2, Pallas kernels, attend_back_call(): pl.pallas_call(waiting(functools.partial(attend_back_kernel, block, tile,...  92.6 us
    pallas_call x1, Pallas kernels, hand_back_call(): pl.pallas_call(functools.partial(hand_back_kernel, seqs), grid=(1,), in_s...  61 us
    pallas_call x2, Pallas kernels, attend_call(): pl.pallas_call(waiting(functools.partial(attend_kernel, block, tile, len(...  48.6 us
    pallas_call x4, Pallas kernels, slope_call(): pl.pallas_call(waiting(functools.partial(slope_kernel, count, len(terms))...  30.5 us
    pallas_call x1, Pallas kernels, ffn_back_call(): pl.pallas_call(waiting(ffn_back_kernel, 5, deps), grid=(2 * rows // tile,...  16.5 us
    unnamed x52, local copies, waits for them, and re-layouts  11.8 us
  transfers between devices with their start and end apart: 4, of which 0 were waited for; matrix products, arithmetic and copies ran while one was open for 1% of the time, Pallas kernels for 29%

profile of v1, /device:TPU:0, one launch (start us, length us, event | category | flops | bytes accessed | tf_op | source)
XLA Modules:
  0.0 517.4 jit_solution(15888427049595121051)
XLA Ops:
  2.7 1.3 copy.47.refs_2_.refs_8_
  4.3 1.3 copy.48.refs_3_.refs_9_
  6.8 49.0 %gather0.1 = (bf16[512,1024]{1,0:T(8,128)(2,1)}, bf16[1024,1024]{1,0:T(8,128)(2,1)}, bf16[1024,512]{1,0:T(8,128)(2,1)}, bf16[1024,512]{1,0:T(8,128)(2,1)}, bf16[...) custom-call(f32[4,1024]{1,0:T(4,128)} %pad_maximum_fusion.1.refs_0_,, ...), custom_call_target="tpu_custom_call" | custom-call | tf_op jit(solution)/shard_map/gather0/pallas_call | solution.py:465
  58.6 24.4 %attend.2 = (bf16[512,1024]{1,0:T(8,128)(2,1)}, bf16[512,1024]{1,0:T(8,128)(2,1)}, bf16[1024,512]{1,0:T(8,128)(2,1)}, f32[8,2,512]{2,1,0:T(2,128)}) custom-call(s32[16]{0:T(128)} %copy-done.21, s32[8,2]{1,0:T(8,128)} %copy.50.refs_1_, bf16[1024,512]{1,0:T(8,128)(2,1)} %get-tuple-element.72.refs_2_, bf16[512,1024]{1,0:T(8,128)(2,1)} %bitcast.76, ...), custom_call_target="tpu_custom_call" | custom-call | flops 12884901888 | bytes 8388608 | tf_op jit(solution)/shard_map/attend/pallas_call | solution.py:624
  83.0 52.7 %gather1.1 = (bf16[512,1024]{1,0:T(8,128)(2,1)}, bf16[1024,1024]{1,0:T(8,128)(2,1)}, bf16[1024,512]{1,0:T(8,128)(2,1)}, bf16[1024,512]{1,0:T(8,128)(2,1)}, bf16[...) custom-call(f32[4,1024]{1,0:T(4,128)} %pad_maximum_fusion.1.refs_0_,, ...), custom_call_target="tpu_custom_call" | custom-call | tf_op jit(solution)/shard_map/gather1/pallas_call | solution.py:465
  135.7 24.3 %attend.3 = (bf16[512,1024]{1,0:T(8,128)(2,1)}, bf16[512,1024]{1,0:T(8,128)(2,1)}, bf16[1024,512]{1,0:T(8,128)(2,1)}, f32[8,2,512]{2,1,0:T(2,128)}) custom-call(s32[16]{0:T(128)} %copy-done.21, s32[8,2]{1,0:T(8,128)} %copy.50.refs_1_, bf16[1024,512]{1,0:T(8,128)(2,1)} %get-tuple-element.82.refs_2_, bf16[512,1024]{1,0:T(8,128)(2,1)} %bitcast.77, ...), custom_call_target="tpu_custom_call" | custom-call | flops 12884901888 | bytes 8388608 | tf_op jit(solution)/shard_map/attend/pallas_call | solution.py:624
  160.0 1.0 copy-done.5
  160.9 46.2 %attend_back.2 = (bf16[1024,512]{1,0:T(8,128)(2,1)}, bf16[2048,512]{1,0:T(8,128)(2,1)}, bf16[2048,512]{1,0:T(8,128)(2,1)}, f32[8,512]{1,0:T(8,128)}) custom-call(s32[16]{0:T(128)} %copy-done.21, s32[8,2]{1,0:T(8,128)} %copy.50.refs_1_, bf16[1024,512]{1,0:T(8,128)(2,1)} %get-tuple-element.82.refs_2_, bf16[512,1024]{1,0:T(8,128)(2,1)} %get-tuple-element.83.refs_3_.refs_7_, ...), custom_call_target="tpu_custom_call" | custom-call | flops 25769803776 | bytes 16777216 | tf_op jit(solution)/shard_map/attend_back/pallas_call | solution.py:737
  207.1 61.0 %hand_back.1 = (bf16[512,1024]{1,0:T(8,128)(2,1)}, bf16[512,1024]{1,0:T(8,128)(2,1)}, bf16[4,2,128,1024]{3,2,1,0:T(8,128)(2,1)}, f32[8,1024]{1,0:T(8,128)}) custom-call(f32[2,1024]{1,0:T(2,128)} %get-tuple-element.185.refs_0_.refs_10_, f32[2,1024]{1,0:T(2,128)} %get-tuple-element.186.refs_8_.refs_1_, bf16[2048,512]{1,0:T(8,128)(2,1)} %get-tuple-element.90.refs_2_, ...), custom_call_target="tpu_custom_call" | custom-call | tf_op jit(solution)/shard_map/hand_back/pallas_call | solution.py:1099
  268.2 10.9 %down_slope.1 = (bf16[4,128,2048]{2,1,0:T(8,128)(2,1)}, bf16[4,128,2048]{2,1,0:T(8,128)(2,1)}) custom-call(s32[8]{0:T(128)} %stack.53.refs_0_, bf16[512,1024]{1,0:T(8,128)(2,1)} %get-tuple-element.100.refs_1_.refs_2_.refs_3_.refs_4_.refs_0_.refs_7_, bf16[512,1024]{1,0:T(8,128)(2,1)} %get-tuple-element.100.refs_1_.refs_2_.refs_3_.refs_4_.refs_0_.refs_7_, ...), custom_call_target="tpu_custom_call" | custom-call | flops 4294967296 | bytes 10485760 | tf_op jit(solution)/shard_map/down_slope/pallas_call | solution.py:943
  279.1 5.3 %output_slope.1 = (bf16[4,128,512]{2,1,0:T(8,128)(2,1)}, bf16[4,128,512]{2,1,0:T(8,128)(2,1)}) custom-call(s32[8]{0:T(128)} %stack.53.refs_0_, bf16[512,1024]{1,0:T(8,128)(2,1)} %get-tuple-element.100.refs_1_.refs_2_.refs_3_.refs_4_.refs_0_.refs_7_, bf16[512,1024]{1,0:T(8,128)(2,1)} %get-tuple-element.100.refs_1_.refs_2_.refs_3_.refs_4_.refs_0_.refs_7_, ...), custom_call_target="tpu_custom_call" | custom-call | flops 1073741824 | bytes 4194304 | tf_op jit(solution)/shard_map/output_slope/pallas_call | solution.py:943
  284.3 16.5 %feed_forward_back.1 = (bf16[512,1024]{1,0:T(8,128)(2,1)}, bf16[512,1024]{1,0:T(8,128)(2,1)}, bf16[1024,2048]{1,0:T(8,128)(2,1)}, f32[1,2048]{1,0:T(1,128)}) custom-call(bf16[512,1024]{1,0:T(8,128)(2,1)} %get-tuple-element.100.refs_1_.refs_2_.refs_3_.refs_4_.refs_0_.refs_7_, ...), custom_call_target="tpu_custom_call" | custom-call | flops 8589934592 | bytes 20971520 | tf_op jit(solution)/shard_map/feed_forward_back/pallas_call | solution.py:503
  300.9 7.4 %up_slope.2 = (bf16[4,128,1024]{2,1,0:T(8,128)(2,1)}, bf16[4,128,1024]{2,1,0:T(8,128)(2,1)}) custom-call(s32[8]{0:T(128)} %stack.52.refs_0_, bf16[1024,1024]{1,0:T(8,128)(2,1)} %get-tuple-element.102.refs_1_.refs_2_.refs_3_.refs_4_, bf16[1024,1024]{1,0:T(8,128)(2,1)} %get-tuple-element.102.refs_1_.refs_2_.refs_3_.refs_4_, ...), custom_call_target="tpu_custom_call" | custom-call | flops 2147483648 | bytes 6291456 | tf_op jit(solution)/shard_map/up_slope/pallas_call | solution.py:943
  308.2 6.9 %up_slope.3 = (bf16[4,128,1024]{2,1,0:T(8,128)(2,1)}, bf16[4,128,1024]{2,1,0:T(8,128)(2,1)}) custom-call(s32[8]{0:T(128)} %stack.52.refs_0_, bf16[1024,1024]{1,0:T(8,128)(2,1)} %get-tuple-element.102.refs_1_.refs_2_.refs_3_.refs_4_, bf16[1024,1024]{1,0:T(8,128)(2,1)} %get-tuple-element.102.refs_1_.refs_2_.refs_3_.refs_4_, ...), custom_call_target="tpu_custom_call" | custom-call | flops 2147483648 | bytes 6291456 | tf_op jit(solution)/shard_map/up_slope/pallas_call | solution.py:943
  315.2 1.1 collective-permute-start.3
  316.3 0.9 collective-permute-start.2
  317.2 2.3 collective-permute-start.1
  319.5 46.4 %attend_back.3 = (bf16[1024,512]{1,0:T(8,128)(2,1)}, bf16[2048,512]{1,0:T(8,128)(2,1)}, bf16[2048,512]{1,0:T(8,128)(2,1)}, f32[8,512]{1,0:T(8,128)}) custom-call(s32[16]{0:T(128)} %copy-done.21, s32[8,2]{1,0:T(8,128)} %copy.50.refs_1_, bf16[1024,512]{1,0:T(8,128)(2,1)} %get-tuple-element.82.refs_2_, ...), custom_call_target="tpu_custom_call" | custom-call | flops 25769803776 | bytes 16777216 | tf_op jit(solution)/shard_map/attend_back/pallas_call | solution.py:737
  365.9 0.7 slice.57
  367.5 1.3 copy-done.4
  369.1 134.7 %tail.1 = (f32[512,128]{1,0:T(8,128)}, f32[3,128,512]{2,1,0:T(8,128)}, f32[2048,128]{1,0:T(8,128)}, f32[128,2048]{1,0:T(8,128)}, bf16[4,2,128,1024]{3,2,1,0:T(8,128)(2,1)}, /*index=5*/f32[80,128]{1,0:T(8,128)}) custom-call(bf16[1024,512]{1,0:T(8,128)(2,1)} %get-tuple-element.109.refs_0_, bf16[2048,512]{1,0:T(8,128)(2,1)} %get-tuple-element.110.refs_1_, ...), custom_call_target="tpu_custom_call" | custom-call | tf_op jit(solution)/shard_map/tail/pallas_call | solution.py:1376
  503.8 0.7 slice_bitcast_fusion
  504.6 1.3 fusion.5
  505.9 0.7 slice.62
  506.6 1.3 slice.64
  509.6 1.3 copy.68
  510.9 1.0 copy-done.3
  512.0 1.3 copy.69
  513.6 0.9 copy.70
  514.5 0.7 copy.71
  515.2 1.0 copy.72
  516.2 1.0 copy.73
  (81 shorter events, 9.3 us)
Async XLA Ops:
  0.6 0.7 copy-start
  2.0 54.0 %copy-start.21 = (s32[16]{0:T(128)}, s32[16]{0:T(128)S(1)}, u32[]{:S(2)}) copy-start(s32[16]{0:T(128)S(1)} %gather_fusion) | copy-start | bytes 196
  4.1 1.5 copy-start.16
  4.1 2.1 copy-start.12
  4.1 2.1 copy-start.13
  4.1 2.1 copy-start.17
  4.1 2.1 copy-start.18
  6.8 51.1 %copy-start.19 = (f32[1,1024]{1,0:T(1,128)S(1)}, f32[1,1024]{1,0:T(1,128)}, u32[]{:S(2)}) copy-start(f32[1,1024]{1,0:T(1,128)} %param.29) | copy-start | bytes 12292
  6.8 51.1 %copy-start.20 = (f32[1,1024]{1,0:T(1,128)S(1)}, f32[1,1024]{1,0:T(1,128)}, u32[]{:S(2)}) copy-start(f32[1,1024]{1,0:T(1,128)} %param.25) | copy-start | bytes 12292
  55.9 104.0 %collective-permute-start = (bf16[512,1024]{1,0:T(8,128)(2,1)}, bf16[512,1024]{1,0:T(8,128)(2,1)S(1)}, u32[]{:S(2)}, u32[]{:S(2)}) collective-permute-start(bf16[512,1024]{1,0:T(8,128)(2,1)} %get-tuple-element.83.refs_3_.refs_7_), channel_id=1, source_target_pairs={{0,1},{1,0},{2,3},{3,2},{4,5},{5,4},{6,7},{7,6},{8,9},{9,8},{10,11... | collective-permute-start | bytes 3145736 | tf_op jit(solution)/shard_map/ppermute | solution.py:1541
  159.9 1.0 copy-start.5
  315.2 52.3 %collective-permute-start.3 = (bf16[4,128,1024]{2,1,0:T(8,128)(2,1)}, bf16[4,128,1024]{2,1,0:T(8,128)(2,1)S(1)}, u32[]{:S(2)}, u32[]{:S(2)}) collective-permute-start(bf16[4,128,1024]{2,1,0:T(8,128)(2,1)} %get-tuple-element.122), channel_id=1, source_target_pairs={{0,4},{2,6},{4,0},{6,2},{8,12},{10,14},{12,8},{14,10},{1,5},{3,7},... | collective-permute-start | bytes 3145736 | tf_op jit(solution)/shard_map/ppermute | solution.py:1545
  316.3 51.2 %collective-permute-start.2 = (bf16[4,128,1024]{2,1,0:T(8,128)(2,1)}, bf16[4,128,1024]{2,1,0:T(8,128)(2,1)}, u32[]{:S(2)}, u32[]{:S(2)}) collective-permute-start(bf16[4,128,1024]{2,1,0:T(8,128)(2,1)} %get-tuple-element.121), channel_id=1, source_target_pairs={{0,4},{2,6},{4,0},{6,2},{8,12},{10,14},{12,8},{14,10},{1,5},{3,7},... | collective-permute-start | bytes 3145736 | tf_op jit(solution)/shard_map/ppermute | solution.py:1545
  317.2 50.2 %collective-permute-start.1 = (bf16[4,128,2048]{2,1,0:T(8,128)(2,1)}, bf16[4,128,2048]{2,1,0:T(8,128)(2,1)S(1)}, u32[]{:S(2)}, u32[]{:S(2)}) collective-permute-start(bf16[4,128,2048]{2,1,0:T(8,128)(2,1)} %get-tuple-element.120), channel_id=1, source_target_pairs={{0,2},{2,0},{4,6},{6,4},{8,10},{10,8},{12,14},{14,12},{1,3},{3,1},... | collective-permute-start | bytes 6291464 | tf_op jit(solution)/shard_map/ppermute | solution.py:1545
  319.5 47.2 %copy-start.15 = (f32[1,2048]{1,0:T(1,128)S(1)}, f32[1,2048]{1,0:T(1,128)}, u32[]{:S(2)}) copy-start(f32[1,2048]{1,0:T(1,128)} %get-tuple-element.118) | copy-start | bytes 24580
  319.5 47.2 %copy-start.14 = (f32[8,1024]{1,0:T(8,128)S(1)}, f32[8,1024]{1,0:T(8,128)}, u32[]{:S(2)}) copy-start(f32[8,1024]{1,0:T(8,128)} %get-tuple-element.116) | copy-start | bytes 98308
  367.4 1.7 copy-start.6
  367.5 1.4 copy-start.4
  369.1 140.5 %copy-start.2 = (bf16[4,2,128,1024]{3,2,1,0:T(8,128)(2,1)S(1)}, bf16[4,2,128,1024]{3,2,1,0:T(8,128)(2,1)}, u32[]{:S(2)}) copy-start(bf16[4,2,128,1024]{3,2,1,0:T(8,128)(2,1)} %get-tuple-element.99) | copy-start | bytes 6291460
  505.9 5.1 copy-start.11
  509.6 2.3 copy-start.3
  512.0 1.7 copy-start.9
  512.0 2.5 copy-start.10
  512.0 3.2 copy-start.8
  513.6 2.6 copy-start.7
  514.5 2.7 copy-start.1

commit v2 on v1

--- a/solution.py
+++ b/solution.py
@@ -16,6 +16,7 @@
 STACK = 4
 GROUP = STACK * HEAD
 KEY_TILE = 512
+HALF_TILE = KEY_TILE // 2
 VMEM_LIMIT = 60 * 1024 * 1024
 BF16 = jnp.bfloat16
 F32 = jnp.float32
@@ -354,7 +355,7 @@
         to_far[c] = traffic.send(far0.at[at(c)], far1.at[at(c)], far_s.at[c], far_r.at[c], other_core)
 
     n_st, k_st, v_st, q_st, part0_st, part1_st = near_stage[:6]
-    half = rows // 2
+    half = block
 
     def near_rows(ref, part, value, base=0):
         ref[base + part * half : base + (part + 1) * half] = value
@@ -405,28 +406,19 @@
         far_stage[1][cut] = turn(dot(low, w[1]) + b_joint_ref[1:2], *turns).astype(BF16)
         far_stage[2][cut] = (dot(low, w[2]) + b_joint_ref[2:3]).astype(BF16)
 
-    arrive(0)
-    arrive(1)
-    copies[0].wait()
-    for c in (0, 1):
+    for c in range(seqs):
+        arrive(c)
+        if c == 0:
+            copies[0].wait()
+        else:
+            arrive_far(c - 1)
         to_core[c].wait_recv()
-    low = near_joint(0)
-    if not first:
-        arrive(2)
-    copies[1].wait()
-    copies[2].wait()
-    near_ffn(0, low)
-    if first:
-        arrive(2)
-    arrive(3)
-    arrive_far(0)
-    arrive_far(1)
-    for c in (2, 3):
-        to_core[c].wait_recv()
-    low = near_joint(1)
-    arrive_far(2)
-    near_ffn(1, low)
-    arrive_far(3)
+        low = near_joint(c)
+        if c == 0:
+            copies[1].wait()
+            copies[2].wait()
+        near_ffn(c, low)
+    arrive_far(seqs - 1)
     stores = [pltpu.make_async_copy(own, own_out, store.at[0])]
     stores += [pltpu.make_async_copy(a, b, store.at[1 + n]) for n, (a, b) in enumerate(zip(near_stage, near_outs))]
     for copy in stores:
@@ -570,13 +562,15 @@
         spots = spots_of(places_ref, step, tile, block, (rows, 128), 0)
 
         def attend_to(count):
-            open_end = (count - 1) * KEY_TILE if tile == block else 0
+            length = count * HALF_TILE
+            open_end = length - HALF_TILE if tile == block else 0
+            spans = [(start, min(KEY_TILE, length - start)) for start in range(0, length, KEY_TILE)]
             tops = []
             for g, lane in enumerate(lanes):
                 top = None
-                for start in range(0, count * KEY_TILE, KEY_TILE):
-                    scores = dot_nt(heads[g], keys[start : start + KEY_TILE, lane])
-                    for column in range(0, KEY_TILE, 128):
+                for start, extent in spans:
+                    scores = dot_nt(heads[g], keys[start : start + extent, lane])
+                    for column in range(0, extent, 128):
                         piece = scores[:, column : column + 128]
                         if start + column >= open_end:
                             spot = start + column + lax.broadcasted_iota(jnp.int32, piece.shape, 1)
@@ -586,13 +580,13 @@
                 tops.append(jnp.broadcast_to(jnp.max(top, axis=1, keepdims=True), (rows, 128)))
             for g, lane in enumerate(lanes):
                 mass, total = None, None
-                for start in range(0, count * KEY_TILE, KEY_TILE):
+                for start, extent in spans:
                     raised = []
-                    for column in range(start, start + KEY_TILE, 128):
+                    for column in range(start, start + extent, 128):
                         piece = jnp.exp(scores_ref[g, :, column : column + 128] - tops[g])
                         mass = piece if mass is None else mass + piece
                         raised.append(piece.astype(BF16))
-                    term = dot(jnp.concatenate(raised, axis=1), values[start : start + KEY_TILE, lane])
+                    term = dot(jnp.concatenate(raised, axis=1), values[start : start + extent, lane])
                     total = term if total is None else total + term
                 mass = jnp.broadcast_to(jnp.sum(mass, axis=1, keepdims=True), (rows, 128))
                 total = total * jnp.concatenate([1.0 / mass] * (GROUP // 128), axis=1)
@@ -605,7 +599,7 @@
                 for a in range(STACK):
                     lse_ref[step, g : g + 1, a * tile : (a + 1) * tile] = lse[a * tile : (a + 1) * tile].T[0:1]
 
-        for count in range(1, keys.shape[0] // KEY_TILE + 1):
+        for count in range(1, keys.shape[0] // HALF_TILE + 1):
             pl.when(limits_ref[step, 1] == count)(functools.partial(attend_to, count))
         return 0
 
@@ -682,9 +676,9 @@
         lse = [lse_ref[step, g : g + 1, :] for g in range(groups)]
         total[...] = jnp.zeros_like(total)
 
-        def key_step(masked, index, carry):
+        def key_step(masked, extent, index, carry):
             start = pl.multiple_of(index * KEY_TILE, KEY_TILE)
-            cut = pl.ds(start, KEY_TILE)
+            cut = pl.ds(start, extent)
             for g, lane in enumerate(lanes):
                 scores = dot_nt(keys[cut, lane], heads[g])
                 if masked:
@@ -698,8 +692,14 @@
                 total[lane, :] += dot(keys_t[lane, cut], d_scores)
             return carry
 
-        lax.fori_loop(0, limits_ref[step, 0], functools.partial(key_step, False), 0)
-        lax.fori_loop(limits_ref[step, 0], limits_ref[step, 1], functools.partial(key_step, True), 0)
+        whole_tiles = limits_ref[step, 1] // 2
+        lax.fori_loop(0, limits_ref[step, 0], functools.partial(key_step, False, KEY_TILE), 0)
+        lax.fori_loop(limits_ref[step, 0], whole_tiles, functools.partial(key_step, True, KEY_TILE), 0)
+
+        @pl.when(limits_ref[step, 1] % 2 == 1)
+        def _():
+            key_step(True, HALF_TILE, whole_tiles, 0)
+
         for lane in lanes:
             picked = [total[lane, :][a * HEAD : (a + 1) * HEAD, a * tile : (a + 1) * tile] for a in range(STACK)]
             d_queries[mine, lane] = jnp.concatenate(picked, axis=0).T
@@ -956,6 +956,150 @@
         ),
         name=name,
     )(owners, *ins, *deps)
+
+
+class Sums:
+    def __init__(self, masks, slots, send, receive, remote, totals):
+        self.masks, self.slots, self.send, self.receive = masks, slots, send, receive
+        self.remote, self.totals = remote, totals
+        self.steps = [0] * len(masks)
+        self.running = [None] * len(masks)
+        self.kept = [None] * len(masks)
+        self.first = [sum(len(m) for m in masks[:c]) for c in range(len(masks))]
+
+    def launch(self, c, kept, sent):
+        step = self.steps[c]
+        number = self.first[c] + step
+        self.kept[c] = kept
+        self.running[c] = self.remote(
+            sent, self.slots[c][step], self.send.at[number], self.receive.at[number], self.masks[c][step]
+        )
+
+    def halve(self, c, pieces, count):
+        self.launch(c, pieces, pieces.at[pl.ds(count // 2, count // 2)])
+
+    def go_on(self, c):
+        self.running[c].wait_recv()
+        slot = self.slots[c][self.steps[c]]
+        count = slot.shape[0]
+        total = self.kept[c][:count].astype(F32) + slot[...].astype(F32)
+        self.steps[c] += 1
+        if self.steps[c] == len(self.masks[c]):
+            self.totals[c](total[0])
+            return
+        self.kept[c][:count] = total.astype(BF16)
+        self.halve(c, self.kept[c], count)
+
+
+def ffn_slopes_kernel(late, early, *refs):
+    refs = list(refs)
+    take = lambda count: [refs.pop(0) for _ in range(count)]
+    sources, outs, (sums_ref,) = take(8), take(8), take(1)
+    held = take(8)
+    g0, g1, active, mixture, down, slope, up, second = held
+    d, o, u, hidden, second0, second1, d_z, o_y = take(8)
+    load, store, side_s, side_r = refs
+    me = lax.axis_index("ctx")
+    rows, width = g0.shape
+    units = up.shape[1]
+    size = 1 << len(late)
+    half, quarter = size // 2, size // 4
+    share = width // size
+    count = 4
+    traffic = Traffic()
+    loads = [pltpu.make_async_copy(a, b, load.at[n]) for n, (a, b) in enumerate(zip(sources, held))]
+    for copy in loads:
+        copy.start()
+    chip, plane = {"ctx": exchanged(me, late[0])}, {"ctx": exchanged(me, early[0])}
+    greet([chip, plane])
+
+    def pieces(left, right, target, cut, masks):
+        owners = mask_order(masks)
+        for start in range(0, size, count):
+            spots = [pl.ds(pl.multiple_of(exchanged(me, m) * share, share), share) for m in owners[start : start + count]]
+            total = tn(jnp.concatenate([left(spot) for spot in spots], axis=1), right).astype(BF16)
+            for index in range(count):
+                target[start + index, :, cut] = total[index * share : (index + 1) * share]
+
+    def of_g(spot):
+        return jnp.concatenate([g0[:, spot], g1[:, spot]], axis=0)
+
+    def back(part, ref, target):
+        upstream = ref[...]
+        mine = slice(part * rows, (part + 1) * rows)
+        total = None
+        for start in range(0, units, 512):
+            cut = slice(start, start + 512)
+            d_hidden = (dot_nt(upstream, down[cut, :]) * slope[mine, cut].astype(F32)).astype(BF16)
+            hidden[mine, cut] = d_hidden
+            short = jnp.sum(d_hidden.astype(F32), axis=0, keepdims=True)
+            sums_ref[:, cut] = short if part == 0 else sums_ref[:, cut] + short
+            term = dot_nt(d_hidden, up[:, cut])
+            total = term if total is None else total + term
+        target[...] = total.astype(BF16)
+
+    for n in (0, 1, 2):
+        loads[n].wait()
+    cuts = [slice(0, units // 2), slice(units // 2, units)]
+    on_the_way = []
+    for n, cut in enumerate(cuts):
+        pieces(of_g, active[:, cut], d, cut, early)
+        on_the_way.append(
+            traffic.send(
+                d.at[pl.ds(half, half), :, cut], d_z.at[:, :, cut], side_s.at[n], side_r.at[n], plane
+            )
+        )
+    for n in range(3, 8):
+        loads[n].wait()
+    pieces(of_g, mixture[...], o, slice(0, mixture.shape[1]), late)
+    side = traffic.send(o.at[pl.ds(half, half)], o_y, side_s.at[2], side_r.at[2], chip)
+    back(0, g0, second0)
+    back(1, g1, second1)
+    side.wait_recv()
+    for index in range(half):
+        o[index] = (o[index].astype(F32) + o_y[index].astype(F32)).astype(BF16)
+    for cut in cuts:
+        pieces(lambda spot: second[:, spot], hidden[:, cut], u, cut, late)
+    stores = [o.at[pl.ds(0, quarter)], o.at[pl.ds(quarter, quarter)], u.at[pl.ds(0, half)], u.at[pl.ds(half, half)]]
+    stores += [second0, second1]
+    copies = [pltpu.make_async_copy(a, b, store.at[n]) for n, (a, b) in enumerate(zip(stores, outs))]
+    for copy in copies:
+        copy.start()
+    for copy, cut in zip(on_the_way, cuts):
+        copy.wait_recv()
+        for index in range(half):
+            d[index, :, cut] = (d[index, :, cut].astype(F32) + d_z[index, :, cut].astype(F32)).astype(BF16)
+    stores = [d.at[pl.ds(0, quarter)], d.at[pl.ds(quarter, quarter)]]
+    more = [pltpu.make_async_copy(a, b, store.at[6 + n]) for n, (a, b) in enumerate(zip(stores, outs[6:]))]
+    for copy in more:
+        copy.start()
+    traffic.finish()
+    for copy in copies + more:
+        copy.wait()
+
+
+def ffn_slopes_call(g_pair, active, mixture, w_down, slope, w_up, second_in, late, early, number):
+    ins = (*g_pair, active, mixture, w_down, slope, w_up, second_in)
+    rows, width = g_pair[0].shape
+    units, local = w_up.shape[1], mixture.shape[1]
+    size = 1 << len(late)
+    half, quarter, share = size // 2, size // 4, width // size
+    part = (rows, width)
+    out = [(quarter, share, local)] * 2 + [(half, share, units)] * 2 + [part] * 2 + [(quarter, share, units)] * 2
+    scratch = [x.shape for x in ins] + [(size, share, units), (size, share, local), (size, share, units)]
+    scratch += [(2 * rows, units), part, part, (half, share, units), (half, share, local)]
+    return pl.pallas_call(
+        functools.partial(ffn_slopes_kernel, late, early),
+        grid=(1,),
+        in_specs=anywhere(len(ins)),
+        out_specs=anywhere(len(out)) + [whole((1, units))],
+        out_shape=[shape_of(*x) for x in out] + [shape_of(1, units, dtype=F32)],
+        scratch_shapes=[pltpu.VMEM(x, BF16) for x in scratch]
+        + [pltpu.SemaphoreType.DMA((8,)), pltpu.SemaphoreType.DMA((8,))]
+        + carrier_semaphores(3),
+        compiler_params=params_of(collective_id=number, has_side_effects=True),
+        name="ffn_slopes",
+    )(*ins)
 
 
 def hand_back_kernel(seqs, *refs):
@@ -1108,48 +1252,14 @@
     )(gains, shifts, *sources, attn[1], ffn[1])
 
 
-class Sums:
-    def __init__(self, masks, slots, send, receive, remote, totals):
-        self.masks, self.slots, self.send, self.receive = masks, slots, send, receive
-        self.remote, self.totals = remote, totals
-        self.steps = [0] * len(masks)
-        self.running = [None] * len(masks)
-        self.kept = [None] * len(masks)
-        self.first = [sum(len(m) for m in masks[:c]) for c in range(len(masks))]
-
-    def launch(self, c, kept, sent):
-        step = self.steps[c]
-        number = self.first[c] + step
-        self.kept[c] = kept
-        self.running[c] = self.remote(
-            sent, self.slots[c][step], self.send.at[number], self.receive.at[number], self.masks[c][step]
-        )
-
-    def halve(self, c, pieces, count):
-        self.launch(c, pieces, pieces.at[pl.ds(count // 2, count // 2)])
-
-    def go_on(self, c):
-        self.running[c].wait_recv()
-        slot = self.slots[c][self.steps[c]]
-        count = slot.shape[0]
-        total = self.kept[c][:count].astype(F32) + slot[...].astype(F32)
-        self.steps[c] += 1
-        if self.steps[c] == len(self.masks[c]):
-            self.totals[c](total[0])
-            return
-        self.kept[c][:count] = total.astype(BF16)
-        self.halve(c, self.kept[c], count)
-
-
-def tail_kernel(masks, *refs):
-    late, early = masks
+def tail_kernel(late, early, *refs):
     (dq_in, dk_in, dv_in, w_in, near_in, far_in, h_in, g_in, second0_in, second1_in, gains_ref, words_in, o0_in, o1_in,
-     d0_in, d1_in, ua0_in, ua1_in, ub0_in, ub1_in) = refs[:20]
-    o_out, joint_out, down_out, up_out, home_ref, words_out = refs[20:26]
-    (dq, dk, dv, w, near, far, h, g, second0, second1, o0, d0, d1, ua0, ua1, ub0, ub1, jq, jk, jv,
-     far1, far1_got, sums, arrived, near0, near1, near1_got, d_own, words, other_words) = refs[26:56]
-    slots = refs[56:74]
-    load, chain_send, chain_receive, side_send, side_receive, word_send, word_receive = refs[74:]
+     u0_in, u1_in, d0_in, d1_in) = refs[:18]
+    o_out, joint_out, down_out, up_out, home_ref, words_out = refs[18:24]
+    (dq, dk, dv, w, near, far, h, g, second0, second1, o0, u0, u1, d0, d1, jq, jk, jv,
+     far1, far1_got, sums, arrived, near0, near1, near1_got, d_own, words, other_words) = refs[24:52]
+    slots = refs[52:66]
+    load, chain_send, chain_receive, side_send, side_receive, word_send, word_receive, part_send, part_receive = refs[66:]
     me, core = lax.axis_index("ctx"), lax.axis_index("tp")
     size = words.shape[0]
     rows, width = h.shape
@@ -1175,21 +1285,30 @@
         return send(source, target, side_send.at[number], side_receive.at[number], other_core)
 
     loads = {}
-    order = (
-        ("d0", d0_in, d0), ("d1", d1_in, d1), ("ua0", ua0_in, ua0), ("ua1", ua1_in, ua1), ("ub0", ub0_in, ub0),
-        ("ub1", ub1_in, ub1), ("dk", dk_in, dk), ("dv", dv_in, dv), ("w", w_in, w), ("dq", dq_in, dq), ("near", near_in, near),
-        ("far", far_in, far), ("o0", o0_in, o0), ("h", h_in, h), ("g", g_in, g), ("second0", second0_in, second0),
-    )
-    for number, (name, source, target) in enumerate(order):
-        loads[name] = pltpu.make_async_copy(source, target, load.at[number])
-        loads[name].start()
-
+
+    def start_loads(first, items):
+        for number, (name, source, target) in enumerate(items):
+            loads[name] = pltpu.make_async_copy(source, target, load.at[first + number])
+            loads[name].start()
+
+    upper, lower = pl.ds(chip_rows, chip_rows), pl.ds(0, chip_rows)
+    start_loads(0, (("dk", dk_in.at[upper], dk.at[upper]), ("dv", dv_in.at[upper], dv.at[upper]), ("w", w_in, w)))
     barrier = pltpu.get_barrier_semaphore()
     for mask in range(1, size):
         pl.semaphore_signal(barrier, inc=1, device_id=at_ctx(mask), device_id_type=pl.DeviceIdType.MESH)
     pl.semaphore_signal(barrier, inc=1, device_id=other_core, device_id_type=pl.DeviceIdType.MESH)
     pl.semaphore_wait(barrier, size)
 
+    for name in ("dk", "dv", "w"):
+        loads[name].wait()
+    start_loads(
+        3,
+        (
+            ("u0", u0_in, u0), ("u1", u1_in, u1), ("dq", dq_in, dq), ("dk", dk_in.at[lower], dk.at[lower]),
+            ("dv", dv_in.at[lower], dv.at[lower]), ("h", h_in, h), ("g", g_in, g), ("second0", second0_in, second0),
+            ("near", near_in, near), ("far", far_in, far), ("o0", o0_in, o0), ("d0", d0_in, d0), ("d1", d1_in, d1),
+        ),
+    )
     units = up_out.shape[1]
 
     def put_output(total):
@@ -1204,18 +1323,15 @@
 
         return write
 
-    def put_up(start):
-        def write(total):
-            up_out[:, start : start + units // 2] = total
-
-        return write
-
-    chains = [late, late, late, late, early[1:], early[1:], late[1:]]
+    def put_up(total):
+        up_out[...] = total
+
+    chains = [late[1:], late, late, late, late[1:], early[2:]]
     parts, used = [], 0
     for chain in chains:
         parts.append(slots[used : used + len(chain)])
         used += len(chain)
-    totals = [put_output, put_joint(0), put_joint(1), put_joint(2), put_up(0), put_up(units // 2), put_down]
+    totals = [put_output, put_joint(0), put_joint(1), put_joint(2), put_up, put_down]
     run = Sums(
         chains, parts, chain_send, chain_receive,
         lambda source, target, first, second, mask: send(source, target, first, second, at_ctx(mask)), totals,
@@ -1230,12 +1346,6 @@
             kept[index] = (kept[index].astype(F32) + other[index].astype(F32)).astype(BF16)
         run.halve(c, kept, kept.shape[0])
 
-    ready(6, d0, d1, ("d0", "d1"))
-    ready(4, ua0, ua1, ("ua0", "ua1"))
-    ready(5, ub0, ub1, ("ub0", "ub1"))
-    for name in ("dk", "dv", "w"):
-        loads[name].wait()
-
     def from_far(start):
         cut = slice(start, start + rows)
         return dot_nt(dk[cut], w[1]) + dot_nt(dv[cut], w[2])
@@ -1245,8 +1355,14 @@
     mine = from_far(chip_rows)
     swap.wait_recv()
     sums[...] = (mine + far1_got[...].astype(F32)).astype(BF16)
-    arrival = send(sums, arrived, side_send.at[2], side_receive.at[2], at_ctx(1))
-    loads["dq"].wait()
+    blocks = [*range(seqs // 2, seqs), *range(seqs // 2 - 1, -1, -1)]
+    arrivals = {}
+    for s in blocks:
+        cut = pl.ds(s * block, block)
+        arrivals[s] = send(sums.at[cut], arrived.at[cut], part_send.at[s], part_receive.at[s], at_ctx(1))
+    ready(4, u0, u1, ("u0", "u1"))
+    for name in ("dq", "dk", "dv", "h", "g", "second0"):
+        loads[name].wait()
     loads["near"].wait()
     loads["far"].wait()
     loads["o0"].wait()
@@ -1257,11 +1373,36 @@
     near1[...] = from_near(slice(rows, chip_rows)).astype(BF16)
     near_swap = to_core(near1, near1_got, 3)
     near0[...] = from_near(slice(0, rows)).astype(BF16)
-    run.go_on(0)
+    second_swap.wait_recv()
+    near_swap.wait_recv()
+    gradients = [jnp.zeros((1, width), F32) for _ in range(5)]
+    home = {}
+
+    def norm_back(s):
+        cut = slice(s * block, (s + 1) * block)
+        scaled, inverse = normalize(h[cut].astype(F32))
+        upstream = g[cut].astype(F32)
+        arrivals[s].wait_recv()
+        d_first = near0[cut].astype(F32) + near1_got[cut].astype(F32) + arrived[cut].astype(F32)
+        d_second = second0[cut].astype(F32) + second1[cut].astype(F32)
+        for row, term in enumerate((d_first * scaled, d_first, d_second * scaled, d_second, upstream)):
+            gradients[row] = gradients[row] + jnp.sum(term, axis=0, keepdims=True)
+        d_scaled = d_first * gains_ref[0:1] + d_second * gains_ref[1:2]
+        middle = jnp.mean(d_scaled, axis=-1, keepdims=True)
+        along = jnp.mean(d_scaled * scaled, axis=-1, keepdims=True)
+        d_own[cut] = (upstream + inverse * (d_scaled - middle - scaled * along)).astype(BF16)
+        source, place = d_own.at[pl.ds(s * block, block)], home_ref.at[seq, core]
+        if s == 0:
+            home[s] = pltpu.make_async_copy(source, place, load.at[16])
+            home[s].start()
+        else:
+            home[s] = send(source, place, side_send.at[4 + s], side_receive.at[4 + s], at_ctx(s * chips))
+
     share = width // size
     count = 4
     owners = mask_order(late)
-    for t, (target, grad) in enumerate(((jq, dq), (jk, dk), (jv, dv))):
+
+    def joint_slope(t, target, grad):
         for start in range(0, size, count):
             spots = [pl.ds(pl.multiple_of(exchanged(me, m) * share, share), share) for m in owners[start : start + count]]
             total = tn(jnp.concatenate([near[:, spot] for spot in spots], axis=1), grad[:chip_rows])
@@ -1271,36 +1412,17 @@
             for index in range(count):
                 target[start + index] = low[index * share : (index + 1) * share]
         run.halve(1 + t, target, size)
-        if t == 1:
-            run.go_on(6)
-    for name in ("h", "g", "second0"):
-        loads[name].wait()
-    for copy in (second_swap, near_swap, arrival):
-        copy.wait_recv()
-    gradients = [jnp.zeros((1, width), F32) for _ in range(5)]
-    for s in range(seqs):
-        cut = slice(s * block, (s + 1) * block)
-        scaled, inverse = normalize(h[cut].astype(F32))
-        upstream = g[cut].astype(F32)
-        d_first = near0[cut].astype(F32) + near1_got[cut].astype(F32) + arrived[cut].astype(F32)
-        d_second = second0[cut].astype(F32) + second1[cut].astype(F32)
-        for row, term in enumerate((d_first * scaled, d_first, d_second * scaled, d_second, upstream)):
-            gradients[row] = gradients[row] + jnp.sum(term, axis=0, keepdims=True)
-        d_scaled = d_first * gains_ref[0:1] + d_second * gains_ref[1:2]
-        middle = jnp.mean(d_scaled, axis=-1, keepdims=True)
-        along = jnp.mean(d_scaled * scaled, axis=-1, keepdims=True)
-        d_own[cut] = (upstream + inverse * (d_scaled - middle - scaled * along)).astype(BF16)
-    home = []
-    for s in range(seqs):
-        source = d_own.at[pl.ds(s * block, block)]
-        if s == 0:
-            stay = pltpu.make_async_copy(source, home_ref.at[seq, core], load.at[len(order)])
-            stay.start()
-        else:
-            number = 4 + s
-            home.append(
-                send(source, home_ref.at[seq, core], side_send.at[number], side_receive.at[number], at_ctx(s * chips))
-            )
+
+    joint_slope(0, jq, dq)
+    norm_back(blocks[0])
+    joint_slope(1, jk, dk)
+    norm_back(blocks[1])
+    joint_slope(2, jv, dv)
+    run.go_on(4)
+    run.go_on(0)
+    for s in blocks[2:]:
+        norm_back(s)
+    ready(5, d0, d1, ("d0", "d1"))
     lines = width // 128
     words_out[...] = words_in[...]
     for row in range(5):
@@ -1311,15 +1433,18 @@
         send(words.at[me], words.at[me], word_send.at[mask], word_receive.at[mask], at_ctx(mask))
         for mask in range(1, size)
     ]
-    for c in (0, 4, 1, 2, 5, 3, 1, 6, 4, 2, 0, 5, 3):
+    for c in (0, 1, 4, 1, 2, 2):
         run.go_on(c)
-    stay.wait()
     swaps = []
     for s in range(seqs):
         if s:
-            home[s - 1].wait_recv()
+            home[s].wait_recv()
+        else:
+            home[s].wait()
         place = home_ref.at[exchanged(seq, s), core]
         swaps.append(to_core(place, place, 4 + seqs + s))
+    run.go_on(3)
+    run.go_on(3)
     for copy in word_copies:
         copy.wait_recv()
     total = words[0]
@@ -1333,7 +1458,7 @@
     swap.wait_recv()
     swap.wait_send()
     words_out[pl.ds(0, core_words)] = total[:core_words] + other_words[...]
-    for c in (1, 2, 3):
+    for c in (1, 2, 5, 3):
         run.go_on(c)
     for copy in swaps:
         copy.wait_recv()
@@ -1342,14 +1467,13 @@
             copy.wait_send()
 
 
-def tail_call(grads, w_joint, normals, h, g, seconds, gains, words, core_words, output, down, ups, masks, seqs, number):
-    late, early = masks
+def tail_call(grads, w_joint, normals, h, g, seconds, gains, words, core_words, output, up, down, late, early, seqs, number):
     rows, width = h.shape
     chip_rows, local = grads[0].shape
     size = 1 << len(late)
-    units = down[0].shape[2]
+    units = up[0].shape[2]
     share = width // size
-    ins = (*grads, w_joint, *normals, h, g, *seconds, gains, words, *output, *down, *ups[0], *ups[1])
+    ins = (*grads, w_joint, *normals, h, g, *seconds, gains, words, *output, *up, *down)
     specs = anywhere(len(ins))
     specs[10], specs[11] = whole(gains.shape), whole(words.shape)
     out = [
@@ -1363,18 +1487,18 @@
     half = size // 2
     wide = (rows, width)
     scratch = [x.shape for x in (*grads, w_joint, *normals)] + [wide] * 4 + [output[0].shape]
-    scratch += [down[0].shape] * 2 + [ups[0][0].shape] * 4 + [(size, share, local)] * 3 + [wide] * 8
+    scratch += [x.shape for x in (*up, *down)] + [(size, share, local)] * 3 + [wide] * 8
     scratch = [pltpu.VMEM(shape, BF16) for shape in scratch]
     scratch += [pltpu.VMEM((size, *words.shape), F32), pltpu.VMEM((core_words, 128), F32)]
     for chain, columns, pieces in (
-        (late, local, half), (late, local, half), (late, local, half), (late, local, half),
-        (early[1:], units // 2, half // 2), (early[1:], units // 2, half // 2), (late[1:], units, half // 2),
+        (late[1:], local, half // 2), (late, local, half), (late, local, half), (late, local, half),
+        (late[1:], units, half // 2), (early[2:], units, half // 4),
     ):
         scratch += [pltpu.VMEM((pieces >> step, share, columns), BF16) for step in range(len(chain))]
-    scratch += [pltpu.SemaphoreType.DMA((17,))] + carrier_semaphores(18)
-    scratch += carrier_semaphores(4 + 2 * seqs) + carrier_semaphores(size)
+    scratch += [pltpu.SemaphoreType.DMA((17,))] + carrier_semaphores(14)
+    scratch += carrier_semaphores(4 + 2 * seqs) + carrier_semaphores(size) + carrier_semaphores(seqs)
     return pl.pallas_call(
-        functools.partial(tail_kernel, masks),
+        functools.partial(tail_kernel, late, early),
         grid=(1,),
         in_specs=specs,
         out_specs=[pl.BlockSpec(memory_space=pl.ANY) if n == 4 else whole(x.shape) for n, x in enumerate(out)],
@@ -1606,7 +1730,7 @@
     tile = max(block, 128)
     tile_places = places[: chip_rows // block].reshape(-1, tile // block)
     lowest, highest = jnp.min(tile_places, 1), jnp.max(tile_places, 1)
-    limits = jnp.stack([(lowest * block + 1) // KEY_TILE, (highest * block + block - 1) // KEY_TILE + 1], 1)
+    limits = jnp.stack([(lowest * block + 1) // KEY_TILE, (highest * block + block - 1) // HALF_TILE + 1], 1)
 
     gain_one, shift_one, gain_two, shift_two = first_gain, first_bias, second_gain, second_bias
     w_joint, b_joint = joint_weight[0], joint_bias[0]
@@ -1773,6 +1897,26 @@
             terms = [(jnp.concatenate(g_pair, 0), right, 0)]
         return slope_call(late_owners, terms, name, (0, 1), deps)
 
+    def in_words(values):
+        values = values.reshape(-1)
+        return jnp.pad(values, (0, -values.size % 1024)).reshape(-1, 128)
+
+    if fused:
+        *parts, up_sums = ffn_slopes_call(
+            g_pair, active, mixture, w_down, slope, w_up, second_in, late, early, 2 * sections
+        )
+        o_kept, o_sent, u_kept, u_sent, second0, second1, down_kept, down_sent = parts
+        up_arrived = swap_ctx(u_sent, late[0])
+        down_arrived = swap_ctx(down_sent, early[1])
+        *grads, joint_sums = attention_back(g_pair, kept, (u_kept,))
+        both = in_words(jnp.concatenate([jnp.zeros((5 * width,), F32), moments]))
+        ones = in_words(jnp.concatenate([joint_sums[:3].reshape(-1), up_sums.reshape(-1)]))
+        output_total, joint_total, down_total, up_total, home, small = tail_call(
+            grads, w_joint, normal_parts, own, g_own, [second0, second1], gains, jnp.concatenate([both, ones], 0),
+            both.shape[0], (o_kept, o_sent), (u_kept, up_arrived), (down_kept, down_arrived), late, early, seqs,
+            2 * sections + 1,
+        )
+        return results(section_out, home, small, both.shape[0], joint_total, output_total, up_total, down_total)
     down = of_g(active, "down_slope")
     down_arrived = swap_ctx(down[1], late[0])
     output = of_g(mixture, "output_slope", (down[0],))
@@ -1781,22 +1925,8 @@
     ups.append(slope_call(early_owners, [(second_in, d_hidden, 0)], "up_slope", (1, 2), (ups[0][0],)))
     ups_arrived = [swap_ctx(part[1], early[0]) for part in ups]
     d_queries, d_keys, d_values, joint_sums = attention_back(g_pair, kept, (ups[1][0], output[0]))
-    seconds = [second0, second1]
-
-    def in_words(values):
-        values = values.reshape(-1)
-        return jnp.pad(values, (0, -values.size % 1024)).reshape(-1, 128)
-
     grads = (d_queries, d_keys, d_values)
     ones = in_words(jnp.concatenate([joint_sums[:3].reshape(-1), up_sums.reshape(-1)]))
-    if by_blocks and len(late) == 3:
-        both = in_words(jnp.concatenate([jnp.zeros((5 * width,), F32), moments]))
-        pairs = [(part[0], there) for part, there in zip(ups, ups_arrived)]
-        output_total, joint_total, down_total, up_total, home, small = tail_call(
-            grads, w_joint, normal_parts, own, g_own, seconds, gains, jnp.concatenate([both, ones], 0), both.shape[0],
-            output, (down[0], down_arrived), pairs, (late, early), seqs, 2 * sections,
-        )
-        return results(section_out, home, small, both.shape[0], joint_total, output_total, up_total, down_total)
     sums = far_back(d_keys, d_values, (down_arrived, *ups_arrived))
 
     def halved(pair, arrived):

time: 524 us -> 500 us (0.954)
  Pallas kernels: 486 us -> 466 us
    pallas_call x6 -> x2, Pallas kernels: 182 us -> 169 us  [the longest x1 112 us: tail_call(): pl.pallas_call(functools.partial(tail_kernel, late, early), grid=(1,), in...]
    pallas_call x1, Pallas kernels: 61 us -> 48.8 us  [hand_back_call(): pl.pallas_call(functools.partial(hand_back_kernel, seqs), grid=(1,), in_s...]
    pallas_call x2, Pallas kernels: 92.6 us -> 99.4 us  [attend_back_call(): pl.pallas_call(waiting(functools.partial(attend_back_kernel, block, tile,...]
    unnamed x52 -> x48, local copies, waits for them, and re-layouts: 11.8 us -> 13.2 us
  transfers between devices with their start and end apart: 4 -> 3, of which waited for: 0 -> 0; matrix products, arithmetic and copies ran while one was open for 1% -> 1% of each run, Pallas kernels for 29% -> 30%
where the time goes in v2:
time: 500 us; the launch traced here: 494 us
  Pallas kernels  466 us (93%)
  local copies, waits for them, and re-layouts  23 us (5%)
    pallas_call x1, Pallas kernels, tail_call(): pl.pallas_call(functools.partial(tail_kernel, late, early), grid=(1,), in...  112 us
    pallas_call x2, Pallas kernels, attend_back_call(): pl.pallas_call(waiting(functools.partial(attend_back_kernel, block, tile,...  99.4 us
    pallas_call x2, Pallas kernels, gather_call(): pl.pallas_call(functools.partial(gather_kernel, first, save, seqs), grid=...  97.3 us
    pallas_call x1, Pallas kernels, ffn_slopes_call(): pl.pallas_call(functools.partial(ffn_slopes_kernel, late, early), grid=(1...  56.8 us
    pallas_call x2, Pallas kernels, attend_call(): pl.pallas_call(waiting(functools.partial(attend_kernel, block, tile, len(...  51.2 us
    pallas_call x1, Pallas kernels, hand_back_call(): pl.pallas_call(functools.partial(hand_back_kernel, seqs), grid=(1,), in_s...  48.8 us
    unnamed x48, local copies, waits for them, and re-layouts  13.2 us
  transfers between devices with their start and end apart: 3, of which 0 were waited for; matrix products, arithmetic and copies ran while one was open for 1% of the time, Pallas kernels for 30%

profile of v2, /device:TPU:0, one launch (start us, length us, event | category | flops | bytes accessed | tf_op | source)
XLA Modules:
  0.0 493.6 jit_solution(8573488639195705534)
XLA Ops:
  1.3 0.7 gather_fusion
  2.1 1.3 copy.59
  3.9 1.3 copy.47.refs_2_.refs_8_
  5.4 1.3 copy.48.refs_3_.refs_9_
  6.7 0.6 pad_maximum_fusion.1.refs_0_
  7.4 49.0 %gather0.1 = (bf16[512,1024]{1,0:T(8,128)(2,1)}, bf16[1024,1024]{1,0:T(8,128)(2,1)}, bf16[1024,512]{1,0:T(8,128)(2,1)}, bf16[1024,512]{1,0:T(8,128)(2,1)}, bf16[...) custom-call(f32[4,1024]{1,0:T(4,128)} %pad_maximum_fusion.1.refs_0_,, ...), custom_call_target="tpu_custom_call" | custom-call | tf_op jit(solution)/shard_map/gather0/pallas_call | solution.py:457
  56.5 0.7 copy.50.refs_1_
  57.2 0.6 pad_maximum_fusion.2
  57.8 25.6 %attend.2 = (bf16[512,1024]{1,0:T(8,128)(2,1)}, bf16[512,1024]{1,0:T(8,128)(2,1)}, bf16[1024,512]{1,0:T(8,128)(2,1)}, f32[8,2,512]{2,1,0:T(2,128)}) custom-call(s32[16]{0:T(128)} %copy-done.19, s32[8,2]{1,0:T(8,128)} %copy.50.refs_1_, bf16[1024,512]{1,0:T(8,128)(2,1)} %get-tuple-element.69.refs_2_, bf16[512,1024]{1,0:T(8,128)(2,1)} %bitcast.68, ...), custom_call_target="tpu_custom_call" | custom-call | flops 12884901888 | bytes 8388608 | tf_op jit(solution)/shard_map/attend/pallas_call | solution.py:618
  83.5 48.3 %gather1.1 = (bf16[512,1024]{1,0:T(8,128)(2,1)}, bf16[1024,1024]{1,0:T(8,128)(2,1)}, bf16[1024,512]{1,0:T(8,128)(2,1)}, bf16[1024,512]{1,0:T(8,128)(2,1)}, bf16[...) custom-call(f32[4,1024]{1,0:T(4,128)} %pad_maximum_fusion.1.refs_0_,, ...), custom_call_target="tpu_custom_call" | custom-call | tf_op jit(solution)/shard_map/gather1/pallas_call | solution.py:457
  131.8 25.6 %attend.3 = (bf16[512,1024]{1,0:T(8,128)(2,1)}, bf16[512,1024]{1,0:T(8,128)(2,1)}, bf16[1024,512]{1,0:T(8,128)(2,1)}, f32[8,2,512]{2,1,0:T(2,128)}) custom-call(s32[16]{0:T(128)} %copy-done.19, s32[8,2]{1,0:T(8,128)} %copy.50.refs_1_, bf16[1024,512]{1,0:T(8,128)(2,1)} %get-tuple-element.79.refs_2_, bf16[512,1024]{1,0:T(8,128)(2,1)} %bitcast.69, ...), custom_call_target="tpu_custom_call" | custom-call | flops 12884901888 | bytes 8388608 | tf_op jit(solution)/shard_map/attend/pallas_call | solution.py:618
  157.4 1.0 copy-done.4
  158.4 49.7 %attend_back.2 = (bf16[1024,512]{1,0:T(8,128)(2,1)}, bf16[2048,512]{1,0:T(8,128)(2,1)}, bf16[2048,512]{1,0:T(8,128)(2,1)}, f32[8,512]{1,0:T(8,128)}) custom-call(s32[16]{0:T(128)} %copy-done.19, s32[8,2]{1,0:T(8,128)} %copy.50.refs_1_, bf16[1024,512]{1,0:T(8,128)(2,1)} %get-tuple-element.79.refs_2_, bf16[512,1024]{1,0:T(8,128)(2,1)} %get-tuple-element.80.refs_3_.refs_7_, ...), custom_call_target="tpu_custom_call" | custom-call | flops 25769803776 | bytes 16777216 | tf_op jit(solution)/shard_map/attend_back/pallas_call | solution.py:737
  208.1 48.8 %hand_back.1 = (bf16[512,1024]{1,0:T(8,128)(2,1)}, bf16[512,1024]{1,0:T(8,128)(2,1)}, bf16[4,2,128,1024]{3,2,1,0:T(8,128)(2,1)}, f32[8,1024]{1,0:T(8,128)}) custom-call(f32[2,1024]{1,0:T(2,128)} %get-tuple-element.179.refs_0_.refs_10_, f32[2,1024]{1,0:T(2,128)} %get-tuple-element.180.refs_8_.refs_1_, bf16[2048,512]{1,0:T(8,128)(2,1)} %get-tuple-element.87.refs_2_, ...), custom_call_target="tpu_custom_call" | custom-call | tf_op jit(solution)/shard_map/hand_back/pallas_call | solution.py:1243
  256.9 56.8 %ffn_slopes.1 = (bf16[2,128,512]{2,1,0:T(8,128)(2,1)}, bf16[2,128,512]{2,1,0:T(8,128)(2,1)}, bf16[4,128,2048]{2,1,0:T(8,128)(2,1)}, bf16[4,128,2048]{2,1,0:T(8,1...) custom-call(bf16[512,1024]{1,0:T(8,128)(2,1)} %get-tuple-element.97., ...), custom_call_target="tpu_custom_call" | custom-call | tf_op jit(solution)/shard_map/ffn_slopes/pallas_call | solution.py:1091
  313.9 49.7 %attend_back.3 = (bf16[1024,512]{1,0:T(8,128)(2,1)}, bf16[2048,512]{1,0:T(8,128)(2,1)}, bf16[2048,512]{1,0:T(8,128)(2,1)}, f32[8,512]{1,0:T(8,128)}) custom-call(s32[16]{0:T(128)} %copy-done.19, s32[8,2]{1,0:T(8,128)} %copy.50.refs_1_, bf16[1024,512]{1,0:T(8,128)(2,1)} %get-tuple-element.79.refs_2_, ...), custom_call_target="tpu_custom_call" | custom-call | flops 25769803776 | bytes 16777216 | tf_op jit(solution)/shard_map/attend_back/pallas_call | solution.py:737
  363.6 0.7 slice.57
  364.5 0.6 pad_maximum_fusion.refs_11_
  365.1 1.0 copy-done.5
  366.1 0.7 copy-done.2
  366.8 112.1 %tail.1 = (f32[512,128]{1,0:T(8,128)}, f32[3,128,512]{2,1,0:T(8,128)}, f32[2048,128]{1,0:T(8,128)}, f32[128,2048]{1,0:T(8,128)}, bf16[4,2,128,1024]{3,2,1,0:T(8,128)(2,1)}, /*index=5*/f32[80,128]{1,0:T(8,128)}) custom-call(bf16[1024,512]{1,0:T(8,128)(2,1)} %get-tuple-element.102.refs_0_, bf16[2048,512]{1,0:T(8,128)(2,1)} %get-tuple-element.103.refs_1_, ...), custom_call_target="tpu_custom_call" | custom-call | tf_op jit(solution)/shard_map/tail/pallas_call | solution.py:1500
  479.0 1.3 slice.64
  480.3 0.7 slice.62
  481.0 1.3 fusion.5
  482.3 0.7 slice_bitcast_fusion
  483.0 0.6 reshape.214
  484.7 3.2 copy.68
  488.0 1.3 copy.69
  489.6 0.9 copy.70
  490.5 0.7 copy.71
  491.2 1.0 copy.72
  492.2 1.0 copy.73
  (69 shorter events, 3.3 us)
Async XLA Ops:
  0.6 0.7 copy-start
  2.0 54.5 %copy-start.19 = (s32[16]{0:T(128)}, s32[16]{0:T(128)S(1)}, u32[]{:S(2)}) copy-start(s32[16]{0:T(128)S(1)} %gather_fusion) | copy-start | bytes 196
  5.2 1.5 copy-start.11
  5.2 1.5 copy-start.12
  5.2 1.5 copy-start.15
  5.2 1.5 copy-start.16
  7.4 49.9 %copy-start.17 = (f32[1,1024]{1,0:T(1,128)S(1)}, f32[1,1024]{1,0:T(1,128)}, u32[]{:S(2)}) copy-start(f32[1,1024]{1,0:T(1,128)} %param.29) | copy-start | bytes 12292
  7.4 49.9 %copy-start.18 = (f32[1,1024]{1,0:T(1,128)S(1)}, f32[1,1024]{1,0:T(1,128)}, u32[]{:S(2)}) copy-start(f32[1,1024]{1,0:T(1,128)} %param.25) | copy-start | bytes 12292
  56.4 101.0 %collective-permute-start = (bf16[512,1024]{1,0:T(8,128)(2,1)}, bf16[512,1024]{1,0:T(8,128)(2,1)S(1)}, u32[]{:S(2)}, u32[]{:S(2)}) collective-permute-start(bf16[512,1024]{1,0:T(8,128)(2,1)} %get-tuple-element.80.refs_3_.refs_7_), channel_id=1, source_target_pairs={{0,1},{1,0},{2,3},{3,2},{4,5},{5,4},{6,7},{7,6},{8,9},{9,8},{10,11... | collective-permute-start | bytes 3145736 | tf_op jit(solution)/shard_map/ppermute | solution.py:1665
  157.4 1.0 copy-start.4
  313.7 51.4 %collective-permute-start.2 = (bf16[2,128,2048]{2,1,0:T(8,128)(2,1)}, bf16[2,128,2048]{2,1,0:T(8,128)(2,1)S(1)}, u32[]{:S(2)}, u32[]{:S(2)}) collective-permute-start(bf16[2,128,2048]{2,1,0:T(8,128)(2,1)} %get-tuple-element.116), channel_id=1, source_target_pairs={{0,8},{2,10},{4,12},{6,14},{8,0},{10,2},{12,4},{14,6},{1,9},{3,11}... | collective-permute-start | bytes 3145736 | tf_op jit(solution)/shard_map/ppermute | solution.py:1669
  313.8 51.3 %collective-permute-start.1 = (bf16[4,128,2048]{2,1,0:T(8,128)(2,1)}, bf16[4,128,2048]{2,1,0:T(8,128)(2,1)S(1)}, u32[]{:S(2)}, u32[]{:S(2)}) collective-permute-start(bf16[4,128,2048]{2,1,0:T(8,128)(2,1)} %get-tuple-element.114), channel_id=1, source_target_pairs={{0,2},{2,0},{4,6},{6,4},{8,10},{10,8},{12,14},{14,12},{1,3},{3,1},... | collective-permute-start | bytes 6291464 | tf_op jit(solution)/shard_map/ppermute | solution.py:1669
  313.9 50.5 %copy-start.14 = (f32[1,2048]{1,0:T(1,128)S(1)}, f32[1,2048]{1,0:T(1,128)}, u32[]{:S(2)}) copy-start(f32[1,2048]{1,0:T(1,128)} %get-tuple-element.111) | copy-start | bytes 24580
  313.9 50.5 %copy-start.13 = (f32[8,1024]{1,0:T(8,128)S(1)}, f32[8,1024]{1,0:T(8,128)}, u32[]{:S(2)}) copy-start(f32[8,1024]{1,0:T(8,128)} %get-tuple-element.109) | copy-start | bytes 98308
  365.1 1.0 copy-start.5
  365.1 1.7 copy-start.2
  482.3 5.7 %copy-start.10 = (f32[8,128]{1,0:T(8,128)}, f32[8,128]{1,0:T(8,128)S(1)}, u32[]{:S(2)}) copy-start(f32[8,128]{1,0:T(8,128)S(1)} %get-tuple-element.168) | copy-start | bytes 12292
  484.7 3.2 copy-start.3
  488.0 1.7 copy-start.8
  488.0 2.5 copy-start.9
  489.6 1.6 copy-start.7
  489.6 2.6 copy-start.6
  490.5 2.7 copy-start.1
